TPU v7x, 512 devices: a whole 4x4x16 slice. The times are simulated.
512 devices in a mesh: cfg: 8 (over z_hi, x), col: 64 (over y, z_lo, core).
Axes of the slice: x: 4, y: 4, z: 16 (z_hi: 2, z_lo: 8; z = z_hi * 8 + z_lo), core: 2. Of those that a mesh axis runs over, the one named last changes fastest.
Arguments:
- band_values: bfloat16 [3, 16384, 1024], P(None, ('cfg', 'col')), may hold values from -0.1875 to 0.1875
- initial_vectors: bfloat16 [16384, 1024], P(('cfg', 'col')), may hold values from -0.1875 to 0.1875
- final_vectors: bfloat16 [6144, 16384], P('col', 'cfg'), may hold values from -6 to 6
- band_offsets: int32 [256], P('cfg'), may hold values from 0 to 15360, as said below
Outputs:
- dipole: bfloat16 [3, 6144, 1024], P(None, 'col', 'cfg')
Inputs may be any that keep to these rules, and one draw needn't show every extreme that they name: `band_offsets`: the band of configuration block b begins within 32 of b * 64 + 64 // 2 - 1024 // 2, clipped to the matrix.
All inputs are finite; a program needn't handle non-finite values.
Results may differ from a plain program's by a relative error of at most 0.0049.
Values may be sent and summed in bfloat16 or wider, within the bound.
No kernel may reach another device: no remote copies, remote signals or barrier semaphores. Data moves between devices by JAX's collectives and lax.ppermute only.
A program may use at most 64 MiB of HBM per device.

v0:
```python
import jax
import jax.numpy as jnp
from jax import lax
from jax.sharding import PartitionSpec as P

BLK = 64


def with_halo(array, sides, width):
    for axis, dim in sides:
        peers, length = (lax.axis_size(axis), array.shape[dim])
        up = [(i, (i + 1) % peers) for i in range(peers - 1)]
        down = [(j, i) for i, j in up]
        last = lax.slice_in_dim(array, length - width, length, axis=dim)
        first = lax.slice_in_dim(array, 0, width, axis=dim)
        before = lax.ppermute(last, axis, up)
        after = lax.ppermute(first, axis, down)
        array = jnp.concatenate([before, array, after], axis=dim)
    return array


def shards(band_values, initial_vectors, final_vectors, band_offsets):
    row_count = final_vectors.shape[1]
    band_width = band_values.shape[2]
    half_band = band_width // 2
    columns = final_vectors.shape[0]
    block_count = band_offsets.shape[0]
    group_start = lax.axis_index("cfg") * row_count
    panel = with_halo(final_vectors, (("cfg", 1),), half_band)
    window_starts = band_offsets - group_start + half_band
    windows = jax.vmap(lambda first_col: lax.dynamic_slice_in_dim(panel, first_col, band_width, 1))(
        window_starts
    )
    gathered = lax.all_gather(band_values, "col", axis=1, tiled=True)
    grouped = gathered.reshape(gathered.shape[0], block_count, BLK, band_width)
    applied = jnp.einsum("pbkw,bcw->pcbk", grouped, windows, preferred_element_type=jnp.float32)
    applied = applied.astype(jnp.bfloat16).reshape(gathered.shape[0], columns, row_count)
    running = jnp.einsum(
        "mlg,gs->mls",
        applied,
        lax.all_gather(initial_vectors, "col", axis=0, tiled=True),
        preferred_element_type=jnp.float32,
    )
    return lax.psum_scatter(running, "cfg", scatter_dimension=2, tiled=True).astype(jnp.bfloat16)


def solution(mesh):
    placed = (P(None, ("cfg", "col"), None), P(("cfg", "col"), None), P("col", "cfg"), P("cfg"))
    return jax.shard_map(
        shards, mesh=mesh, in_specs=placed, out_specs=P(None, "col", "cfg"), check_vma=False
    )
```

profile of v0, /device:TPU:8, one launch (start us, length us, event | category | flops | bytes accessed | tf_op | source)
XLA Modules:
  0.0 400.7 jit_solution(14208147318841818115)
XLA Ops:
  8.3 3.4 collective-permute-start
  13.9 4.3 %collective-permute-done.1 = bf16[96,512]{1,0:T(8,128)(2,1)S(1)} collective-permute-done((bf16[96,512]{1,0:T(8,128)(2,1)S(1)}, bf16[96,512]{1,0:T(8,128)(2,1)S(1)}, u32[]{:S(2)}, u32[]{:S(2)}) %collective-permute-start.1) | collective-permute-done | bytes 98336 | tf_op jit(solution)/shard_map/ppermute | solution.py:17
  19.2 65.8 %while.1 = (s32[]{:T(128)}, bf16[96,3072]{1,0:T(8,128)(2,1)S(1)}, s32[32,2]{0,1:T(2,128)S(1)}, bf16[32,96,1024]{2,1,0:T(8,128)(2,1)}, s32[]{:T(128)}) while((s32[]{:T(128)}, bf16[96,3072]{1,0:T(8,128)(2,1)S(1)}, s32[32,2]{0,1:T(2,128)S(1)}, bf16[32,96,1024]{2,1,0:T(8,128)(2,1)}, s32[]{:T(128)}) %tuple.17), condition=%wide.while_cond, body=%wide.while_body.sunk | while | flops 2 | bytes 394329 | solution.py:31
  19.9 1.4 bitcast_dynamic-update-slice_fusion.2
  21.9 1.5 bitcast_dynamic-update-slice_fusion.2
  24.0 1.4 bitcast_dynamic-update-slice_fusion.2
  26.0 1.5 bitcast_dynamic-update-slice_fusion.2
  28.1 1.4 bitcast_dynamic-update-slice_fusion.2
  30.2 1.4 bitcast_dynamic-update-slice_fusion.2
  34.3 1.4 bitcast_dynamic-update-slice_fusion.2
  40.4 1.4 bitcast_dynamic-update-slice_fusion.2
  42.5 1.5 bitcast_dynamic-update-slice_fusion.2
  46.6 1.4 bitcast_dynamic-update-slice_fusion.2
  48.6 1.4 bitcast_dynamic-update-slice_fusion.2
  50.7 1.4 bitcast_dynamic-update-slice_fusion.2
  56.8 1.4 bitcast_dynamic-update-slice_fusion.2
  60.9 1.5 bitcast_dynamic-update-slice_fusion.2
  63.0 1.4 bitcast_dynamic-update-slice_fusion.2
  65.0 1.4 bitcast_dynamic-update-slice_fusion.2
  67.1 1.4 bitcast_dynamic-update-slice_fusion.2
  69.2 1.4 bitcast_dynamic-update-slice_fusion.2
  71.2 1.4 bitcast_dynamic-update-slice_fusion.2
  73.3 1.4 bitcast_dynamic-update-slice_fusion.2
  75.3 1.5 bitcast_dynamic-update-slice_fusion.2
  81.5 1.5 bitcast_dynamic-update-slice_fusion.2
  83.5 1.5 bitcast_dynamic-update-slice_fusion.2
  85.0 64.6 %all-gather.3.cloned.1.call-done = bf16[3,2048,1024]{2,1,0:T(8,128)(2,1)} async-done(((bf16[3,32,1024]{2,1,0:T(8,128)(2,1)}), bf16[3,2048,1024]{2,1,0:T(8,128)(2,1)}) %all-gather.3.cloned.1.call-update) | async-done | bytes 12582928 | tf_op jit(solution)/shard_map/all_gather | solution.py:34
  149.6 8.2 %fusion.10 = bf16[3,96,32,64]{1,3,0,2:T(8,128)(2,1)S(1)} fusion(bf16[3,32,64,1024]{3,2,1,0:T(8,128)(2,1)} %bitcast.27, bf16[32,96,1024]{2,1,0:T(8,128)(2,1)} %get-tuple-element.12), kind=kOutput, calls=%fused_computation.8 | convolution fusion | flops 1208549376 | bytes 20054016 | tf_op jit(solution)/shard_map/pbkw,bcw->pcbk/dot_general | solution.py:36
  158.0 110.8 %all-gather.5.cloned.1.call-done = bf16[2048,1024]{1,0:T(8,128)(2,1)} async-done(((bf16[32,1024]{1,0:T(8,128)(2,1)}), bf16[2048,1024]{1,0:T(8,128)(2,1)}) %all-gather.5.cloned.1.call-update) | async-done | bytes 4194320 | tf_op jit(solution)/shard_map/all_gather | solution.py:41
  268.8 4.6 %fusion.3 = f32[3,96,1024]{2,1,0:T(8,128)} fusion(bf16[3,96,2048]{1,2,0:T(8,128)(2,1)S(1)} %bitcast.26, bf16[2048,1024]{1,0:T(8,128)(2,1)} %all-gather.5.cloned.1.call-done), kind=kOutput, calls=%fused_computation.5 | convolution fusion | flops 1207959552 | bytes 6553600 | tf_op jit(solution)/shard_map/mlg,gs->mls/dot_general | solution.py:38
  273.5 119.2 %reduce-scatter.2.cloned.1.call-done = f32[3,96,128]{2,1,0:T(8,128)} async-done(((f32[3,96,1024]{2,1,0:T(8,128)}), f32[3,96,128]{2,1,0:T(8,128)}) %reduce-scatter.2.cloned.1.call-update) | async-done | bytes 147472 | tf_op jit(solution)/shard_map/reduce_scatter | solution.py:44
  392.6 1.6 convert_element_type.11
  (87 shorter events, 37.5 us)
Async XLA Ops:
  6.5 143.1 %all-gather.3.cloned.1.call-start = ((), (), s32[]{:S(2)}) async-start(), calls=%async_computation.1 | async-start | bytes 12779520 | tf_op jit(solution)/shard_map/all_gather | solution.py:34
  7.3 261.6 %all-gather.5.cloned.1.call-start = ((), (), s32[]{:S(2)}) async-start(), calls=%async_computation.2 | async-start | bytes 4259840 | tf_op jit(solution)/shard_map/all_gather | solution.py:41
  8.3 5.6 %collective-permute-start = (bf16[96,512]{1,0:T(8,128)(2,1)S(1)}, bf16[96,512]{1,0:T(8,128)(2,1)S(1)}, u32[]{:S(2)}, u32[]{:S(2)}) collective-permute-start(bf16[96,512]{1,0:T(8,128)(2,1)S(1)} %get-tuple-element.21), channel_id=1, source_target_pairs={{0,64},{64,128},{128,192},{192,256},{256,320},{320,384},{384,448},... | collective-permute-start | bytes 294920 | tf_op jit(solution)/shard_map/ppermute | solution.py:16
  11.7 6.5 %collective-permute-start.1 = (bf16[96,512]{1,0:T(8,128)(2,1)S(1)}, bf16[96,512]{1,0:T(8,128)(2,1)S(1)}, u32[]{:S(2)}, u32[]{:S(2)}) collective-permute-start(bf16[96,512]{1,0:T(8,128)(2,1)S(1)} %get-tuple-element.22), channel_id=1, source_target_pairs={{64,0},{128,64},{192,128},{256,192},{320,256},{384,320},{448,384},... | collective-permute-start | bytes 294920 | tf_op jit(solution)/shard_map/ppermute | solution.py:17
  13.0 379.6 %reduce-scatter.2.cloned.1.call-start = ((), (), s32[]{:S(2)}) async-start(), calls=%async_computation.3 | async-start | bytes 1327104 | tf_op jit(solution)/shard_map/reduce_scatter | solution.py:44
Sparse Core Ops, SparseCore 0:
  9.5 140.0 all-gather.2
  151.7 117.0 all-gather.4
  273.6 119.0 reduce-scatter.1
where the time goes:
time: 401 us
  waiting for transfers between devices  300 us (75%)
  local copies, waits for them, and re-layouts  66.8 us (17%)
  between operations  13.2 us (3%)
  matrix products  12.9 us (3%)
  starting transfers between devices  4.77 us (1%)
    reduce_scatter x1, waiting for transfers between devices, shards(): lax.psum_scatter(running, 'cfg', scatter_dimension=2, tiled=True)  119 us
    all_gather x1, waiting for transfers between devices, shards(): lax.all_gather(initial_vectors, 'col', axis=0, tiled=True)  111 us
    gather x96, local copies, waits for them, and re-layouts  65.7 us
    all_gather x1, waiting for transfers between devices, shards(): gathered = lax.all_gather(band_values, 'col', axis=1, tiled=True)  64.6 us
    dot_general x1, matrix products, shards(): jnp.einsum('pbkw,bcw->pcbk', grouped, windows, preferred_element_type=jnp...  8.24 us
  transfers between devices with their start and end apart: 5, of which 5 were waited for; matrix products, arithmetic and copies ran while one was open for 19% of the time, Pallas kernels for 0%

commit v1 on v0

v1 whole, which is shorter than its diff:
```python
import functools

import jax
import jax.numpy as jnp
from jax import lax
from jax.experimental import pallas as pl
from jax.experimental.pallas import tpu as pltpu
from jax.sharding import Mesh
from jax.sharding import PartitionSpec as P

BLK = 64
HALF = 512
AXES = ("zh", "x", "y", "zl", "core")
ORDER = (0, 4, 2, 6, 1, 5, 3, 7)


def roll_kernel(start_ref, band_ref, vec_ref, out_ref):
    comps = band_ref.shape[0]
    for p in range(comps):
        rows = band_ref[p].astype(jnp.float32)
        out_ref[p] = pltpu.roll(rows, start_ref[0], 1).astype(out_ref.dtype)
    out_ref[comps] = vec_ref[...]


def product_kernel(starts_ref, panel_ref, *refs):
    pieces, out_ref, band_s, vec_s = refs[:-3], refs[-3], refs[-2], refs[-1]
    p = pl.program_id(0)
    rows, width = pieces[0].shape[1:]
    lane = lax.broadcasted_iota(jnp.int32, (rows, HALF), 1)
    for n, ref in enumerate(pieces):
        at = pl.ds(n * rows, rows)
        start = starts_ref[n // 2]
        low = ref[p, :, :HALF]
        zero = jnp.zeros_like(low)
        band_s[at, :HALF] = jnp.where(lane >= start, low, zero)
        band_s[at, HALF:width] = ref[p, :, HALF:]
        band_s[at, width:] = jnp.where(lane < start, low, zero)
        vec_s[at, :] = ref[3]
    quarters, lines = panel_ref.shape[:2]
    panel = panel_ref[...].reshape(quarters * lines, panel_ref.shape[2])
    applied = lax.dot_general(
        panel, band_s[...], (((1,), (1,)), ((), ())), preferred_element_type=jnp.float32
    ).astype(jnp.bfloat16)
    sums = jnp.dot(applied, vec_s[...], preferred_element_type=jnp.float32)
    out_ref[...] = sums.reshape(out_ref.shape).astype(out_ref.dtype)


def shards(band_values, initial_vectors, final_vectors, band_offsets):
    comps, own_rows, width = band_values.shape
    lines, row_count = final_vectors.shape
    vectors = initial_vectors.shape[1]
    zh, x, y, zl = (lax.axis_index(a) for a in AXES[:4])
    panel_start = (zh * 4 + x) * row_count + (y - 1) * HALF
    order = jnp.array(ORDER, jnp.int32) ^ zl
    starts = jnp.take(band_offsets, y * 8 + order, mode="clip") - panel_start

    up = [(i, i + 1) for i in range(7)]
    down = [(i + 1, i) for i in range(7)]
    before = lax.ppermute(final_vectors[:, row_count - HALF :], ("zh", "x"), up)
    after = lax.ppermute(final_vectors[:, :HALF], ("zh", "x"), down)

    own = pl.pallas_call(
        roll_kernel,
        out_shape=jax.ShapeDtypeStruct((comps + 1, own_rows, width), jnp.bfloat16),
        in_specs=[
            pl.BlockSpec(memory_space=pltpu.SMEM),
            pl.BlockSpec(memory_space=pltpu.VMEM),
            pl.BlockSpec(memory_space=pltpu.VMEM),
        ],
        out_specs=pl.BlockSpec(memory_space=pltpu.VMEM),
        name="roll",
    )(starts, band_values, initial_vectors)

    def along_z(block, step):
        return lax.ppermute(block, "zl", [(i, i ^ step) for i in range(8)])

    def other_core(block):
        return lax.ppermute(block, "core", [(0, 1), (1, 0)])

    blocks = [own]
    for step in (4, 2, 1):
        blocks = blocks + [along_z(b, step) for b in blocks]
    pieces = []
    for b in blocks:
        pieces += [b, other_core(b)]

    wide = jnp.concatenate([before, final_vectors, after], axis=1)
    windows = jnp.stack([wide[:, HALF * k : HALF * (k + 3)] for k in range(4)])
    panel = lax.all_to_all(windows, "y", 0, 0)

    vmem = pl.BlockSpec(memory_space=pltpu.VMEM)
    depth = len(pieces) * own_rows
    sums = pl.pallas_call(
        product_kernel,
        grid=(comps,),
        out_shape=jax.ShapeDtypeStruct((4, comps, lines, vectors), jnp.bfloat16),
        in_specs=[pl.BlockSpec(memory_space=pltpu.SMEM), vmem] + [vmem] * len(pieces),
        out_specs=pl.BlockSpec((4, 1, lines, vectors), lambda p: (0, p, 0, 0)),
        scratch_shapes=[
            pltpu.VMEM((depth, 3 * HALF), jnp.bfloat16),
            pltpu.VMEM((depth, vectors), jnp.bfloat16),
        ],
        compiler_params=pltpu.CompilerParams(vmem_limit_bytes=32 * 1024 * 1024),
        cost_estimate=pl.CostEstimate(
            flops=2 * comps * 4 * lines * depth * (3 * HALF + vectors), bytes_accessed=12_000_000, transcendentals=0
        ),
        name="product",
    )(starts, panel, *pieces)

    def add_up(parts):
        return jnp.sum(parts.astype(jnp.float32), axis=0)

    over_y = add_up(lax.all_to_all(sums, "y", 0, 0)).astype(jnp.bfloat16)
    over_y = over_y.reshape(comps, lines, 2, 4, vectors // 8).transpose(3, 2, 0, 1, 4)
    over_x = add_up(lax.all_to_all(over_y, "x", 0, 0))
    mine = jnp.where(zh == 0, over_x[0], over_x[1])
    theirs = jnp.where(zh == 0, over_x[1], over_x[0]).astype(jnp.bfloat16)
    got = lax.ppermute(theirs, "zh", [(0, 1), (1, 0)])
    return (mine + got.astype(jnp.float32)).astype(jnp.bfloat16)


def solution(mesh):
    fine = Mesh(mesh.devices.reshape(2, 4, 4, 8, 2), AXES)
    cfg, col = AXES[:2], AXES[2:]
    placed = (P(None, AXES, None), P(AXES, None), P(col, cfg), P(cfg))
    return jax.shard_map(
        shards, mesh=fine, in_specs=placed, out_specs=P(None, col, cfg), check_vma=False
    )
```

time: 401 us -> 176 us (0.44)
  the two profiles are of different devices: /device:TPU:8 before, /device:TPU:2 now
where the time goes in v1:
time: 176 us; the launch traced here: 175 us
  starting transfers between devices  83.2 us (47%)
  waiting for transfers between devices  34.2 us (19%)
  blocking collectives  34.2 us (19%)
  local copies, waits for them, and re-layouts  11.7 us (7%)
  Pallas kernels  6.83 us (4%)
  other arithmetic  4.56 us (3%)
    all_to_all x1, blocking collectives, shards(): over_y = add_up(lax.all_to_all(sums, 'y', 0, 0)).astype(jnp.bfloat16)  34.2 us
    ppermute x7, starting transfers between devices, along_z(): return lax.ppermute(block, 'zl', [(i, i ^ step) for i in range(8)])  24.5 us
    ppermute x7, waiting for transfers between devices, along_z(): return lax.ppermute(block, 'zl', [(i, i ^ step) for i in range(8)])  20.2 us
    all_to_all x1, starting transfers between devices, shards(): over_x = add_up(lax.all_to_all(over_y, 'x', 0, 0))  17.3 us
    ppermute x8, starting transfers between devices, other_core(): return lax.ppermute(block, 'core', [(0, 1), (1, 0)])  16.3 us
    ppermute x1, starting transfers between devices, shards(): got = lax.ppermute(theirs, 'zh', [(0, 1), (1, 0)])  11.5 us
    unnamed x29, local copies, waits for them, and re-layouts  8.28 us
    all_to_all x1, waiting for transfers between devices, shards(): over_x = add_up(lax.all_to_all(over_y, 'x', 0, 0))  8.27 us
  transfers between devices with their start and end apart: 20, of which 5 were waited for; matrix products, arithmetic and copies ran while one was open for 2% of the time, Pallas kernels for 1%

profile of v1, /device:TPU:2, one launch (start us, length us, event | category | flops | bytes accessed | tf_op | source)
XLA Modules:
  0.0 175.0 jit_solution(16085981764225647912)
XLA Ops:
  0.0 1.0 fusion.3
  1.0 3.4 %collective-permute-start = (bf16[96,512]{1,0:T(8,128)(2,1)S(1)}, bf16[96,512]{1,0:T(8,128)(2,1)S(1)}, u32[]{:S(2)}, u32[]{:S(2)}) collective-permute-start(bf16[96,512]{1,0:T(8,128)(2,1)S(1)} %get-tuple-element.9), channel_id=1, source_target_pairs={{0,64},{64,128},{128,192},{192,256},{256,320},{320,384},{384,448},... | collective-permute-start | bytes 294920 | tf_op jit(solution)/shard_map/ppermute | solution.py:59
  4.4 5.7 %collective-permute-start.1 = (bf16[96,512]{1,0:T(8,128)(2,1)S(1)}, bf16[96,512]{1,0:T(8,128)(2,1)S(1)}, u32[]{:S(2)}, u32[]{:S(2)}) collective-permute-start(bf16[96,512]{1,0:T(8,128)(2,1)S(1)} %get-tuple-element.10), channel_id=1, source_target_pairs={{64,0},{128,64},{192,128},{256,192},{320,256},{384,320},{448,384},... | collective-permute-start | bytes 294920 | tf_op jit(solution)/shard_map/ppermute | solution.py:60
  12.0 1.8 %roll.1.refs_0_ = bf16[4,32,1024]{2,1,0:T(8,128)(2,1)} custom-call(s32[8]{0:T(128)} %broadcast_subtract_fusion.start_ref.starts_ref, bf16[3,32,1024]{2,1,0:T(8,128)(2,1)} %band_ref.1, bf16[32,1024]{1,0:T(8,128)(2,1)} %vec_ref.1), custom_call_target="tpu_custom_call" | custom-call | tf_op jit(solution)/shard_map/roll/pallas_call | solution.py:62
  13.8 5.8 %collective-permute-start.3 = (bf16[4,32,1024]{2,1,0:T(8,128)(2,1)}, bf16[4,32,1024]{2,1,0:T(8,128)(2,1)S(1)}, u32[]{:S(2)}, u32[]{:S(2)}) collective-permute-start(bf16[4,32,1024]{2,1,0:T(8,128)(2,1)} %roll.1.refs_0_), channel_id=1, source_target_pairs={{0,8},{2,10},{4,12},{6,14},{8,0},{10,2},{12,4},{14,6},{1,9},{3,11}... | collective-permute-start | bytes 786440 | tf_op jit(solution)/shard_map/ppermute | solution.py:75
  19.7 1.2 pad_maximum_fusion
  20.9 4.6 %all-to-all-start = ((bf16[4,96,1536]{2,1,0:T(8,128)(2,1)}), bf16[4,96,1536]{2,1,0:T(8,128)(2,1)S(1)}, u32[]{:S(2)}, u32[]{:S(2)}) async-start(bf16[4,96,1536]{2,1,0:T(8,128)(2,1)} %pad_maximum_fusion), calls=%async_computation | async-start | bytes 2359296 | tf_op jit(solution)/shard_map/all_to_all | solution.py:89
  25.5 3.8 %collective-permute-start.9 = (bf16[4,32,1024]{2,1,0:T(8,128)(2,1)S(1)}, bf16[4,32,1024]{2,1,0:T(8,128)(2,1)S(1)}, u32[]{:S(2)}, u32[]{:S(2)}) collective-permute-start(bf16[4,32,1024]{2,1,0:T(8,128)(2,1)S(1)} %copy-done.1), channel_id=1, source_target_pairs={{0,2},{2,0},{4,6},{6,4},{8,10},{10,8},{12,14},{14,12},{1,3},{3,1},... | collective-permute-start | bytes 786440 | tf_op jit(solution)/shard_map/ppermute | solution.py:75
  29.3 5.2 %collective-permute-start.5 = (bf16[4,32,1024]{2,1,0:T(8,128)(2,1)S(1)}, bf16[4,32,1024]{2,1,0:T(8,128)(2,1)S(1)}, u32[]{:S(2)}, u32[]{:S(2)}) collective-permute-start(bf16[4,32,1024]{2,1,0:T(8,128)(2,1)S(1)} %copy-done.1), channel_id=1, source_target_pairs={{0,4},{2,6},{4,0},{6,2},{8,12},{10,14},{12,8},{14,10},{1,5},{3,7},... | collective-permute-start | bytes 786440 | tf_op jit(solution)/shard_map/ppermute | solution.py:75
  34.5 1.9 %collective-permute-start.2 = (bf16[4,32,1024]{2,1,0:T(8,128)(2,1)S(1)}, bf16[4,32,1024]{2,1,0:T(8,128)(2,1)S(1)}, u32[]{:S(2)}, u32[]{:S(2)}) collective-permute-start(bf16[4,32,1024]{2,1,0:T(8,128)(2,1)S(1)} %copy-done.1), channel_id=1, source_target_pairs={{0,1},{1,0},{2,3},{3,2},{4,5},{5,4},{6,7},{7,6},{8,9},{9,8},{10,11... | collective-permute-start | bytes 786440 | tf_op jit(solution)/shard_map/ppermute | solution.py:78
  36.4 6.0 %collective-permute-done.3.refs_2_ = bf16[4,32,1024]{2,1,0:T(8,128)(2,1)S(1)} collective-permute-done((bf16[4,32,1024]{2,1,0:T(8,128)(2,1)}, bf16[4,32,1024]{2,1,0:T(8,128)(2,1)S(1)}, u32[]{:S(2)}, u32[]{:S(2)}) %collective-permute-start.3) | collective-permute-done | bytes 262176 | tf_op jit(solution)/shard_map/ppermute | solution.py:75
  42.5 1.9 %collective-permute-start.7 = (bf16[4,32,1024]{2,1,0:T(8,128)(2,1)S(1)}, bf16[4,32,1024]{2,1,0:T(8,128)(2,1)S(1)}, u32[]{:S(2)}, u32[]{:S(2)}) collective-permute-start(bf16[4,32,1024]{2,1,0:T(8,128)(2,1)S(1)} %collective-permute-done.3.refs_2_), channel_id=1, source_target_pairs={{0,4},{2,6},{4,0},{6,2},{8,12},{10,14},{12,8},{14,10},{1,5},{3,7},... | collective-permute-start | bytes 786440 | tf_op jit(solution)/shard_map/ppermute | solution.py:75
  44.4 1.9 %collective-permute-start.10 = (bf16[4,32,1024]{2,1,0:T(8,128)(2,1)S(1)}, bf16[4,32,1024]{2,1,0:T(8,128)(2,1)S(1)}, u32[]{:S(2)}, u32[]{:S(2)}) collective-permute-start(bf16[4,32,1024]{2,1,0:T(8,128)(2,1)S(1)} %collective-permute-done.9.refs_8_), channel_id=1, source_target_pairs={{0,1},{1,0},{2,3},{3,2},{4,5},{5,4},{6,7},{7,6},{8,9},{9,8},{10,11... | collective-permute-start | bytes 786440 | tf_op jit(solution)/shard_map/ppermute | solution.py:78
  46.3 13.3 %collective-permute-done.5.refs_4_ = bf16[4,32,1024]{2,1,0:T(8,128)(2,1)S(1)} collective-permute-done((bf16[4,32,1024]{2,1,0:T(8,128)(2,1)S(1)}, bf16[4,32,1024]{2,1,0:T(8,128)(2,1)S(1)}, u32[]{:S(2)}, u32[]{:S(2)}) %collective-permute-start.5) | collective-permute-done | bytes 262176 | tf_op jit(solution)/shard_map/ppermute | solution.py:75
  59.7 1.9 %collective-permute-start.13 = (bf16[4,32,1024]{2,1,0:T(8,128)(2,1)S(1)}, bf16[4,32,1024]{2,1,0:T(8,128)(2,1)S(1)}, u32[]{:S(2)}, u32[]{:S(2)}) collective-permute-start(bf16[4,32,1024]{2,1,0:T(8,128)(2,1)S(1)} %collective-permute-done.5.refs_4_), channel_id=1, source_target_pairs={{0,2},{2,0},{4,6},{6,4},{8,10},{10,8},{12,14},{14,12},{1,3},{3,1},... | collective-permute-start | bytes 786440 | tf_op jit(solution)/shard_map/ppermute | solution.py:75
  61.6 3.9 %collective-permute-start.11 = (bf16[4,32,1024]{2,1,0:T(8,128)(2,1)S(1)}, bf16[4,32,1024]{2,1,0:T(8,128)(2,1)S(1)}, u32[]{:S(2)}, u32[]{:S(2)}) collective-permute-start(bf16[4,32,1024]{2,1,0:T(8,128)(2,1)S(1)} %collective-permute-done.3.refs_2_), channel_id=1, source_target_pairs={{0,2},{2,0},{4,6},{6,4},{8,10},{10,8},{12,14},{14,12},{1,3},{3,1},... | collective-permute-start | bytes 786440 | tf_op jit(solution)/shard_map/ppermute | solution.py:75
  65.5 1.9 %collective-permute-start.6 = (bf16[4,32,1024]{2,1,0:T(8,128)(2,1)S(1)}, bf16[4,32,1024]{2,1,0:T(8,128)(2,1)S(1)}, u32[]{:S(2)}, u32[]{:S(2)}) collective-permute-start(bf16[4,32,1024]{2,1,0:T(8,128)(2,1)S(1)} %collective-permute-done.5.refs_4_), channel_id=1, source_target_pairs={{0,1},{1,0},{2,3},{3,2},{4,5},{5,4},{6,7},{7,6},{8,9},{9,8},{10,11... | collective-permute-start | bytes 786440 | tf_op jit(solution)/shard_map/ppermute | solution.py:78
  67.4 1.9 %collective-permute-start.15 = (bf16[4,32,1024]{2,1,0:T(8,128)(2,1)S(1)}, bf16[4,32,1024]{2,1,0:T(8,128)(2,1)}, u32[]{:S(2)}, u32[]{:S(2)}) collective-permute-start(bf16[4,32,1024]{2,1,0:T(8,128)(2,1)S(1)} %collective-permute-done.7.refs_6_), channel_id=1, source_target_pairs={{0,2},{2,0},{4,6},{6,4},{8,10},{10,8},{12,14},{14,12},{1,3},{3,1},... | collective-permute-start | bytes 786440 | tf_op jit(solution)/shard_map/ppermute | solution.py:75
  69.4 2.4 %collective-permute-start.4 = (bf16[4,32,1024]{2,1,0:T(8,128)(2,1)S(1)}, bf16[4,32,1024]{2,1,0:T(8,128)(2,1)S(1)}, u32[]{:S(2)}, u32[]{:S(2)}) collective-permute-start(bf16[4,32,1024]{2,1,0:T(8,128)(2,1)S(1)} %collective-permute-done.3.refs_2_), channel_id=1, source_target_pairs={{0,1},{1,0},{2,3},{3,2},{4,5},{5,4},{6,7},{7,6},{8,9},{9,8},{10,11... | collective-permute-start | bytes 786440 | tf_op jit(solution)/shard_map/ppermute | solution.py:78
  71.8 1.9 %collective-permute-start.14 = (bf16[4,32,1024]{2,1,0:T(8,128)(2,1)S(1)}, bf16[4,32,1024]{2,1,0:T(8,128)(2,1)S(1)}, u32[]{:S(2)}, u32[]{:S(2)}) collective-permute-start(bf16[4,32,1024]{2,1,0:T(8,128)(2,1)S(1)} %collective-permute-done.13.refs_12_), channel_id=1, source_target_pairs={{0,1},{1,0},{2,3},{3,2},{4,5},{5,4},{6,7},{7,6},{8,9},{9,8},{10,11... | collective-permute-start | bytes 786440 | tf_op jit(solution)/shard_map/ppermute | solution.py:78
  74.6 1.9 %collective-permute-start.12 = (bf16[4,32,1024]{2,1,0:T(8,128)(2,1)S(1)}, bf16[4,32,1024]{2,1,0:T(8,128)(2,1)S(1)}, u32[]{:S(2)}, u32[]{:S(2)}) collective-permute-start(bf16[4,32,1024]{2,1,0:T(8,128)(2,1)S(1)} %collective-permute-done.11.refs_10_), channel_id=1, source_target_pairs={{0,1},{1,0},{2,3},{3,2},{4,5},{5,4},{6,7},{7,6},{8,9},{9,8},{10,11... | collective-permute-start | bytes 786440 | tf_op jit(solution)/shard_map/ppermute | solution.py:78
  77.2 2.4 %collective-permute-start.8 = (bf16[4,32,1024]{2,1,0:T(8,128)(2,1)S(1)}, bf16[4,32,1024]{2,1,0:T(8,128)(2,1)S(1)}, u32[]{:S(2)}, u32[]{:S(2)}) collective-permute-start(bf16[4,32,1024]{2,1,0:T(8,128)(2,1)S(1)} %collective-permute-done.7.refs_6_), channel_id=1, source_target_pairs={{0,1},{1,0},{2,3},{3,2},{4,5},{5,4},{6,7},{7,6},{8,9},{9,8},{10,11... | collective-permute-start | bytes 786440 | tf_op jit(solution)/shard_map/ppermute | solution.py:78
  79.6 1.9 %collective-permute-start.16 = (bf16[4,32,1024]{2,1,0:T(8,128)(2,1)}, bf16[4,32,1024]{2,1,0:T(8,128)(2,1)}, u32[]{:S(2)}, u32[]{:S(2)}) collective-permute-start(bf16[4,32,1024]{2,1,0:T(8,128)(2,1)} %collective-permute-done.15.refs_14_), channel_id=1, source_target_pairs={{0,1},{1,0},{2,3},{3,2},{4,5},{5,4},{6,7},{7,6},{8,9},{9,8},{10,11... | collective-permute-start | bytes 786440 | tf_op jit(solution)/shard_map/ppermute | solution.py:78
  86.3 0.9 copy-done.8
  87.3 0.9 copy-done.10
  89.2 5.0 %product.1 = bf16[4,3,96,1024]{3,2,1,0:T(8,128)(2,1)S(1)} custom-call(s32[8]{0:T(128)S(1)} %copy-done.2, bf16[4,96,1536]{2,1,0:T(8,128)(2,1)S(1)} %all-to-all-done.panel_ref, bf16[4,32,1024]{2,1,0:T(8,128)(2,1)S(1)} %copy-done.1, bf16[4,32,1024]{2,1,0:T(8,128)(2,1)S(1)} %collective-permute-done.2.refs_1_, ...), custom_call_target="tpu_custom_call" | custom-call | flops 3019898880 | bytes 12000000 | tf_op jit(solution)/shard_map/product/pallas_call | solution.py:93
  94.2 34.2 %all_to_all.15 = bf16[4,3,96,1024]{3,2,1,0:T(8,128)(2,1)S(1)} all-to-all(bf16[4,3,96,1024]{3,2,1,0:T(8,128)(2,1)S(1)} %product.1), channel_id=1, replica_groups=mesh['zh'=2,'x'=4,'y'=4,'zl'=8,'core'=2] {'y'}, dimensions={0} | all-to-all | bytes 4718592 | tf_op jit(solution)/shard_map/all_to_all | solution.py:113
  129.3 1.3 copy.12
  130.6 17.3 %all-to-all-start.2 = ((bf16[4,2,3,96,128]{4,1,3,2,0:T(2,128)(2,1)}), bf16[4,2,3,96,128]{4,1,3,2,0:T(2,128)(2,1)S(1)}, u32[]{:S(2)}, u32[]{:S(2)}) async-start(bf16[4,2,3,96,128]{4,1,3,2,0:T(2,128)(2,1)} %copy.12), calls=%async_computation.2 | async-start | bytes 1179648 | tf_op jit(solution)/shard_map/all_to_all | solution.py:115
  147.9 8.3 %all-to-all-done.2 = bf16[4,2,3,96,128]{4,1,3,2,0:T(2,128)(2,1)S(1)} async-done(((bf16[4,2,3,96,128]{4,1,3,2,0:T(2,128)(2,1)}), bf16[4,2,3,96,128]{4,1,3,2,0:T(2,128)(2,1)S(1)}, u32[]{:S(2)}, u32[]{:S(2)}) %all-to-all-start.2) | async-done | bytes 589856 | tf_op jit(solution)/shard_map/all_to_all | solution.py:115
  157.0 11.5 %collective-permute-start.17 = (bf16[3,96,128]{2,1,0:T(8,128)(2,1)S(1)}, bf16[3,96,128]{2,1,0:T(8,128)(2,1)S(1)}, u32[]{:S(2)}, u32[]{:S(2)}) collective-permute-start(bf16[3,96,128]{2,1,0:T(8,128)(2,1)S(1)} %bitcast.15), channel_id=1, source_target_pairs={{0,256},{256,0},{1,257},{257,1},{2,258},{258,2},{3,259},{259,3},{4... | collective-permute-start | bytes 221192 | tf_op jit(solution)/shard_map/ppermute | solution.py:118
  168.7 5.7 %collective-permute-done.17 = bf16[3,96,128]{2,1,0:T(8,128)(2,1)S(1)} collective-permute-done((bf16[3,96,128]{2,1,0:T(8,128)(2,1)S(1)}, bf16[3,96,128]{2,1,0:T(8,128)(2,1)S(1)}, u32[]{:S(2)}, u32[]{:S(2)}) %collective-permute-start.17) | collective-permute-done | bytes 73760 | tf_op jit(solution)/shard_map/ppermute | solution.py:118
  (54 shorter events, 11.7 us)
Async XLA Ops:
  0.0 10.8 %copy-start = (s32[32]{0:T(128)S(1)}, s32[32]{0:T(128)}, u32[]{:S(2)}) copy-start(s32[32]{0:T(128)} %param.8) | copy-start | bytes 388
  0.0 19.6 %copy-start.13 = (bf16[96,2048]{1,0:T(8,128)(2,1)S(1)}, bf16[96,2048]{1,0:T(8,128)(2,1)}, u32[]{:S(2)}) copy-start(bf16[96,2048]{1,0:T(8,128)(2,1)} %param.7) | copy-start | bytes 1179652
  1.0 18.6 %collective-permute-start = (bf16[96,512]{1,0:T(8,128)(2,1)S(1)}, bf16[96,512]{1,0:T(8,128)(2,1)S(1)}, u32[]{:S(2)}, u32[]{:S(2)}) collective-permute-start(bf16[96,512]{1,0:T(8,128)(2,1)S(1)} %get-tuple-element.9), channel_id=1, source_target_pairs={{0,64},{64,128},{128,192},{192,256},{256,320},{320,384},{384,448},... | collective-permute-start | bytes 294920 | tf_op jit(solution)/shard_map/ppermute | solution.py:59
  4.4 15.2 %collective-permute-start.1 = (bf16[96,512]{1,0:T(8,128)(2,1)S(1)}, bf16[96,512]{1,0:T(8,128)(2,1)S(1)}, u32[]{:S(2)}, u32[]{:S(2)}) collective-permute-start(bf16[96,512]{1,0:T(8,128)(2,1)S(1)} %get-tuple-element.10), channel_id=1, source_target_pairs={{64,0},{128,64},{192,128},{256,192},{320,256},{384,320},{448,384},... | collective-permute-start | bytes 294920 | tf_op jit(solution)/shard_map/ppermute | solution.py:60
  13.8 28.7 %collective-permute-start.3 = (bf16[4,32,1024]{2,1,0:T(8,128)(2,1)}, bf16[4,32,1024]{2,1,0:T(8,128)(2,1)S(1)}, u32[]{:S(2)}, u32[]{:S(2)}) collective-permute-start(bf16[4,32,1024]{2,1,0:T(8,128)(2,1)} %roll.1.refs_0_), channel_id=1, source_target_pairs={{0,8},{2,10},{4,12},{6,14},{8,0},{10,2},{12,4},{14,6},{1,9},{3,11}... | collective-permute-start | bytes 786440 | tf_op jit(solution)/shard_map/ppermute | solution.py:75
  20.9 4.6 %copy-start.1 = (bf16[4,32,1024]{2,1,0:T(8,128)(2,1)S(1)}, bf16[4,32,1024]{2,1,0:T(8,128)(2,1)}, u32[]{:S(2)}) copy-start(bf16[4,32,1024]{2,1,0:T(8,128)(2,1)} %roll.1.refs_0_) | copy-start | bytes 786436
  20.9 63.5 %copy-start.2 = (s32[8]{0:T(128)S(1)}, s32[8]{0:T(128)}, u32[]{:S(2)}) copy-start(s32[8]{0:T(128)} %broadcast_subtract_fusion.start_ref.starts_ref) | copy-start | bytes 100
  20.9 63.5 %all-to-all-start = ((bf16[4,96,1536]{2,1,0:T(8,128)(2,1)}), bf16[4,96,1536]{2,1,0:T(8,128)(2,1)S(1)}, u32[]{:S(2)}, u32[]{:S(2)}) async-start(bf16[4,96,1536]{2,1,0:T(8,128)(2,1)} %pad_maximum_fusion), calls=%async_computation | async-start | bytes 2359296 | tf_op jit(solution)/shard_map/all_to_all | solution.py:89
  25.5 18.9 %collective-permute-start.9 = (bf16[4,32,1024]{2,1,0:T(8,128)(2,1)S(1)}, bf16[4,32,1024]{2,1,0:T(8,128)(2,1)S(1)}, u32[]{:S(2)}, u32[]{:S(2)}) collective-permute-start(bf16[4,32,1024]{2,1,0:T(8,128)(2,1)S(1)} %copy-done.1), channel_id=1, source_target_pairs={{0,2},{2,0},{4,6},{6,4},{8,10},{10,8},{12,14},{14,12},{1,3},{3,1},... | collective-permute-start | bytes 786440 | tf_op jit(solution)/shard_map/ppermute | solution.py:75
  29.3 30.3 %collective-permute-start.5 = (bf16[4,32,1024]{2,1,0:T(8,128)(2,1)S(1)}, bf16[4,32,1024]{2,1,0:T(8,128)(2,1)S(1)}, u32[]{:S(2)}, u32[]{:S(2)}) collective-permute-start(bf16[4,32,1024]{2,1,0:T(8,128)(2,1)S(1)} %copy-done.1), channel_id=1, source_target_pairs={{0,4},{2,6},{4,0},{6,2},{8,12},{10,14},{12,8},{14,10},{1,5},{3,7},... | collective-permute-start | bytes 786440 | tf_op jit(solution)/shard_map/ppermute | solution.py:75
  34.5 31.0 %collective-permute-start.2 = (bf16[4,32,1024]{2,1,0:T(8,128)(2,1)S(1)}, bf16[4,32,1024]{2,1,0:T(8,128)(2,1)S(1)}, u32[]{:S(2)}, u32[]{:S(2)}) collective-permute-start(bf16[4,32,1024]{2,1,0:T(8,128)(2,1)S(1)} %copy-done.1), channel_id=1, source_target_pairs={{0,1},{1,0},{2,3},{3,2},{4,5},{5,4},{6,7},{7,6},{8,9},{9,8},{10,11... | collective-permute-start | bytes 786440 | tf_op jit(solution)/shard_map/ppermute | solution.py:78
  42.5 25.0 %collective-permute-start.7 = (bf16[4,32,1024]{2,1,0:T(8,128)(2,1)S(1)}, bf16[4,32,1024]{2,1,0:T(8,128)(2,1)S(1)}, u32[]{:S(2)}, u32[]{:S(2)}) collective-permute-start(bf16[4,32,1024]{2,1,0:T(8,128)(2,1)S(1)} %collective-permute-done.3.refs_2_), channel_id=1, source_target_pairs={{0,4},{2,6},{4,0},{6,2},{8,12},{10,14},{12,8},{14,10},{1,5},{3,7},... | collective-permute-start | bytes 786440 | tf_op jit(solution)/shard_map/ppermute | solution.py:75
  44.4 25.0 %collective-permute-start.10 = (bf16[4,32,1024]{2,1,0:T(8,128)(2,1)S(1)}, bf16[4,32,1024]{2,1,0:T(8,128)(2,1)S(1)}, u32[]{:S(2)}, u32[]{:S(2)}) collective-permute-start(bf16[4,32,1024]{2,1,0:T(8,128)(2,1)S(1)} %collective-permute-done.9.refs_8_), channel_id=1, source_target_pairs={{0,1},{1,0},{2,3},{3,2},{4,5},{5,4},{6,7},{7,6},{8,9},{9,8},{10,11... | collective-permute-start | bytes 786440 | tf_op jit(solution)/shard_map/ppermute | solution.py:78
  59.7 12.2 %collective-permute-start.13 = (bf16[4,32,1024]{2,1,0:T(8,128)(2,1)S(1)}, bf16[4,32,1024]{2,1,0:T(8,128)(2,1)S(1)}, u32[]{:S(2)}, u32[]{:S(2)}) collective-permute-start(bf16[4,32,1024]{2,1,0:T(8,128)(2,1)S(1)} %collective-permute-done.5.refs_4_), channel_id=1, source_target_pairs={{0,2},{2,0},{4,6},{6,4},{8,10},{10,8},{12,14},{14,12},{1,3},{3,1},... | collective-permute-start | bytes 786440 | tf_op jit(solution)/shard_map/ppermute | solution.py:75
  61.6 13.0 %collective-permute-start.11 = (bf16[4,32,1024]{2,1,0:T(8,128)(2,1)S(1)}, bf16[4,32,1024]{2,1,0:T(8,128)(2,1)S(1)}, u32[]{:S(2)}, u32[]{:S(2)}) collective-permute-start(bf16[4,32,1024]{2,1,0:T(8,128)(2,1)S(1)} %collective-permute-done.3.refs_2_), channel_id=1, source_target_pairs={{0,2},{2,0},{4,6},{6,4},{8,10},{10,8},{12,14},{14,12},{1,3},{3,1},... | collective-permute-start | bytes 786440 | tf_op jit(solution)/shard_map/ppermute | solution.py:75
  65.5 11.0 %collective-permute-start.6 = (bf16[4,32,1024]{2,1,0:T(8,128)(2,1)S(1)}, bf16[4,32,1024]{2,1,0:T(8,128)(2,1)S(1)}, u32[]{:S(2)}, u32[]{:S(2)}) collective-permute-start(bf16[4,32,1024]{2,1,0:T(8,128)(2,1)S(1)} %collective-permute-done.5.refs_4_), channel_id=1, source_target_pairs={{0,1},{1,0},{2,3},{3,2},{4,5},{5,4},{6,7},{7,6},{8,9},{9,8},{10,11... | collective-permute-start | bytes 786440 | tf_op jit(solution)/shard_map/ppermute | solution.py:78
  67.4 12.2 %collective-permute-start.15 = (bf16[4,32,1024]{2,1,0:T(8,128)(2,1)S(1)}, bf16[4,32,1024]{2,1,0:T(8,128)(2,1)}, u32[]{:S(2)}, u32[]{:S(2)}) collective-permute-start(bf16[4,32,1024]{2,1,0:T(8,128)(2,1)S(1)} %collective-permute-done.7.refs_6_), channel_id=1, source_target_pairs={{0,2},{2,0},{4,6},{6,4},{8,10},{10,8},{12,14},{14,12},{1,3},{3,1},... | collective-permute-start | bytes 786440 | tf_op jit(solution)/shard_map/ppermute | solution.py:75
  69.4 12.2 %collective-permute-start.4 = (bf16[4,32,1024]{2,1,0:T(8,128)(2,1)S(1)}, bf16[4,32,1024]{2,1,0:T(8,128)(2,1)S(1)}, u32[]{:S(2)}, u32[]{:S(2)}) collective-permute-start(bf16[4,32,1024]{2,1,0:T(8,128)(2,1)S(1)} %collective-permute-done.3.refs_2_), channel_id=1, source_target_pairs={{0,1},{1,0},{2,3},{3,2},{4,5},{5,4},{6,7},{7,6},{8,9},{9,8},{10,11... | collective-permute-start | bytes 786440 | tf_op jit(solution)/shard_map/ppermute | solution.py:78
  71.8 10.5 %collective-permute-start.14 = (bf16[4,32,1024]{2,1,0:T(8,128)(2,1)S(1)}, bf16[4,32,1024]{2,1,0:T(8,128)(2,1)S(1)}, u32[]{:S(2)}, u32[]{:S(2)}) collective-permute-start(bf16[4,32,1024]{2,1,0:T(8,128)(2,1)S(1)} %collective-permute-done.13.refs_12_), channel_id=1, source_target_pairs={{0,1},{1,0},{2,3},{3,2},{4,5},{5,4},{6,7},{7,6},{8,9},{9,8},{10,11... | collective-permute-start | bytes 786440 | tf_op jit(solution)/shard_map/ppermute | solution.py:78
  74.6 8.4 %collective-permute-start.12 = (bf16[4,32,1024]{2,1,0:T(8,128)(2,1)S(1)}, bf16[4,32,1024]{2,1,0:T(8,128)(2,1)S(1)}, u32[]{:S(2)}, u32[]{:S(2)}) collective-permute-start(bf16[4,32,1024]{2,1,0:T(8,128)(2,1)S(1)} %collective-permute-done.11.refs_10_), channel_id=1, source_target_pairs={{0,1},{1,0},{2,3},{3,2},{4,5},{5,4},{6,7},{7,6},{8,9},{9,8},{10,11... | collective-permute-start | bytes 786440 | tf_op jit(solution)/shard_map/ppermute | solution.py:78
  76.5 0.7 copy-start.3
  77.2 6.5 %collective-permute-start.8 = (bf16[4,32,1024]{2,1,0:T(8,128)(2,1)S(1)}, bf16[4,32,1024]{2,1,0:T(8,128)(2,1)S(1)}, u32[]{:S(2)}, u32[]{:S(2)}) collective-permute-start(bf16[4,32,1024]{2,1,0:T(8,128)(2,1)S(1)} %collective-permute-done.7.refs_6_), channel_id=1, source_target_pairs={{0,1},{1,0},{2,3},{3,2},{4,5},{5,4},{6,7},{7,6},{8,9},{9,8},{10,11... | collective-permute-start | bytes 786440 | tf_op jit(solution)/shard_map/ppermute | solution.py:78
  79.6 4.8 %collective-permute-start.16 = (bf16[4,32,1024]{2,1,0:T(8,128)(2,1)}, bf16[4,32,1024]{2,1,0:T(8,128)(2,1)}, u32[]{:S(2)}, u32[]{:S(2)}) collective-permute-start(bf16[4,32,1024]{2,1,0:T(8,128)(2,1)} %collective-permute-done.15.refs_14_), channel_id=1, source_target_pairs={{0,1},{1,0},{2,3},{3,2},{4,5},{5,4},{6,7},{7,6},{8,9},{9,8},{10,11... | collective-permute-start | bytes 786440 | tf_op jit(solution)/shard_map/ppermute | solution.py:78
  82.3 0.7 copy-start.7
  83.0 0.7 copy-start.9
  84.4 1.0 copy-start.4
  85.4 0.9 copy-start.6
  86.3 0.9 copy-start.8
  87.3 0.9 copy-start.10
  88.2 0.9 copy-start.12
  130.6 25.5 %all-to-all-start.2 = ((bf16[4,2,3,96,128]{4,1,3,2,0:T(2,128)(2,1)}), bf16[4,2,3,96,128]{4,1,3,2,0:T(2,128)(2,1)S(1)}, u32[]{:S(2)}, u32[]{:S(2)}) async-start(bf16[4,2,3,96,128]{4,1,3,2,0:T(2,128)(2,1)} %copy.12), calls=%async_computation.2 | async-start | bytes 1179648 | tf_op jit(solution)/shard_map/all_to_all | solution.py:115
  157.0 17.3 %collective-permute-start.17 = (bf16[3,96,128]{2,1,0:T(8,128)(2,1)S(1)}, bf16[3,96,128]{2,1,0:T(8,128)(2,1)S(1)}, u32[]{:S(2)}, u32[]{:S(2)}) collective-permute-start(bf16[3,96,128]{2,1,0:T(8,128)(2,1)S(1)} %bitcast.15), channel_id=1, source_target_pairs={{0,256},{256,0},{1,257},{257,1},{2,258},{258,2},{3,259},{259,3},{4... | collective-permute-start | bytes 221192 | tf_op jit(solution)/shard_map/ppermute | solution.py:118
  (2 other events, 1.4 us)

commit v2 on v0

v2 whole, which is shorter than its diff:
```python
import functools

import jax
import jax.numpy as jnp
from jax import lax
from jax.experimental import pallas as pl
from jax.experimental.pallas import tpu as pltpu
from jax.sharding import Mesh
from jax.sharding import PartitionSpec as P

BLK = 64
HALF = 512
AXES = ("zh", "x", "y", "zl", "core")
ORDER = (0, 4, 2, 6, 1, 5, 3, 7)
VMEM = pl.BlockSpec(memory_space=pltpu.VMEM)
SMEM = pl.BlockSpec(memory_space=pltpu.SMEM)


def panel_start(row_count):
    zh, x, y = (lax.axis_index(a) for a in AXES[:3])
    return (zh * 4 + x) * row_count + (y - 1) * HALF


def roll_kernel(offsets_ref, band_ref, vec_ref, fin_ref, head_ref, tail_ref, last_ref, first_ref):
    row_count = fin_ref.shape[1]
    start = offsets_ref[lax.axis_index("y") * 8 + lax.axis_index("zl")] - panel_start(row_count)

    def rolled(p):
        return pltpu.roll(band_ref[p].astype(jnp.float32), start, 1).astype(jnp.bfloat16)

    head_ref[0, 0] = vec_ref[...]
    head_ref[0, 1] = rolled(0)
    tail_ref[0, 0] = rolled(1)
    tail_ref[0, 1] = rolled(2)
    last_ref[...] = fin_ref[:, row_count - HALF :]
    first_ref[...] = fin_ref[:, :HALF]


def product_kernel(row_count, count, offsets_ref, panel_ref, *refs):
    vecs, bands, out_ref, band_s, vec_s = refs[:4], refs[4:-3], refs[-3], refs[-2], refs[-1]
    bands = bands or vecs
    p = pl.program_id(0) + (2 - count)
    blocks, _, rows, width = vecs[0].shape
    base, zl = lax.axis_index("y") * 8, lax.axis_index("zl")
    lane = lax.broadcasted_iota(jnp.int32, (rows, HALF), 1)
    for a in range(4):
        for n in range(blocks):
            at = pl.ds((a * blocks + n) * rows, rows)
            start = offsets_ref[base + (zl ^ ORDER[a // 2 * blocks + n])] - panel_start(row_count)
            low = bands[a][n, p, :, :HALF]
            zero = jnp.zeros_like(low)
            band_s[at, :HALF] = jnp.where(lane >= start, low, zero)
            band_s[at, HALF:width] = bands[a][n, p, :, HALF:]
            band_s[at, width:] = jnp.where(lane < start, low, zero)
            vec_s[at, :] = vecs[a][n, 0]
    quarters, lines = panel_ref.shape[:2]
    panel = panel_ref[...].reshape(quarters * lines, panel_ref.shape[2])
    applied = lax.dot_general(
        panel, band_s[...], (((1,), (1,)), ((), ())), preferred_element_type=jnp.float32
    ).astype(jnp.bfloat16)
    sums = jnp.dot(applied, vec_s[...], preferred_element_type=jnp.float32).astype(out_ref.dtype)
    lanes = out_ref.shape[-1]
    for dx in range(4):
        for dy in range(4):
            for dz in range(2):
                out_ref[dx * 4 + dy, 0, dz] = sums[
                    dy * lines : (dy + 1) * lines, (dz * 4 + dx) * lanes : (dz * 4 + dx + 1) * lanes
                ]


def shards(band_values, initial_vectors, final_vectors, band_offsets):
    comps, own_rows, width = band_values.shape
    lines, row_count = final_vectors.shape
    vectors = initial_vectors.shape[1]
    zh = lax.axis_index("zh")
    bf16 = jnp.bfloat16

    half = jax.ShapeDtypeStruct((1, 2, own_rows, width), bf16)
    edge = jax.ShapeDtypeStruct((lines, HALF), bf16)
    head, tail, last, first = pl.pallas_call(
        roll_kernel,
        out_shape=(half, half, edge, edge),
        in_specs=[SMEM, VMEM, VMEM, VMEM],
        out_specs=(VMEM, VMEM, VMEM, VMEM),
        name="roll",
    )(band_offsets, band_values, initial_vectors, final_vectors)

    def along_z(blocks, step):
        return lax.ppermute(blocks, "zl", [(i, i ^ step) for i in range(8)])

    def other_core(blocks):
        return lax.ppermute(blocks, "core", [(0, 1), (1, 0)])

    def gathered(own):
        two = jnp.concatenate([own, along_z(own, 4)])
        near = jnp.concatenate([two, along_z(two, 2)])
        far = along_z(near, 1)
        return [near, other_core(near), far, other_core(far)]

    head_blocks = gathered(head)
    tail_blocks = gathered(tail)

    before = lax.ppermute(last, ("zh", "x"), [(i, i + 1) for i in range(7)])
    after = lax.ppermute(first, ("zh", "x"), [(i + 1, i) for i in range(7)])
    wide = jnp.concatenate([before, final_vectors, after], axis=1)
    windows = jnp.stack([wide[:, HALF * k : HALF * (k + 3)] for k in range(4)])
    panel = lax.all_to_all(windows, "y", 0, 0)

    def product(count, vecs, bands):
        depth = 16 * own_rows
        return pl.pallas_call(
            functools.partial(product_kernel, row_count, count),
            grid=(count,),
            out_shape=jax.ShapeDtypeStruct((16, count, 2, lines, vectors // 8), bf16),
            in_specs=[SMEM, VMEM] + [VMEM] * (len(vecs) + len(bands)),
            out_specs=pl.BlockSpec((16, 1, 2, lines, vectors // 8), lambda p: (0, p, 0, 0, 0)),
            scratch_shapes=[pltpu.VMEM((depth, 3 * HALF), bf16), pltpu.VMEM((depth, vectors), bf16)],
            compiler_params=pltpu.CompilerParams(vmem_limit_bytes=24 * 1024 * 1024),
            cost_estimate=pl.CostEstimate(
                flops=2 * count * 4 * lines * depth * (3 * HALF + vectors),
                bytes_accessed=4_000_000 * count,
                transcendentals=0,
            ),
            name=f"product_{count}",
        )(band_offsets, panel, *vecs, *bands)

    def summed(partial):
        parts = lax.all_to_all(partial, ("x", "y"), 0, 0)
        total = jnp.sum(parts.astype(jnp.float32), axis=0)
        mine = jnp.where(zh == 0, total[:, 0], total[:, 1])
        theirs = jnp.where(zh == 0, total[:, 1], total[:, 0]).astype(bf16)
        got = lax.ppermute(theirs, "zh", [(0, 1), (1, 0)])
        return (mine + got.astype(jnp.float32)).astype(bf16)

    first_sum = summed(product(1, head_blocks, []))
    rest_sum = summed(product(2, head_blocks, tail_blocks))
    return jnp.concatenate([first_sum, rest_sum])


def solution(mesh):
    fine = Mesh(mesh.devices.reshape(2, 4, 4, 8, 2), AXES)
    cfg, col = AXES[:2], AXES[2:]
    placed = (P(None, AXES, None), P(AXES, None), P(col, cfg), P(cfg))
    return jax.shard_map(
        shards, mesh=fine, in_specs=placed, out_specs=P(None, col, cfg), check_vma=False
    )
```

time: 401 us -> 147 us (0.37)
  the two profiles are of different devices: /device:TPU:8 before, /device:TPU:32 now
where the time goes in v2:
time: 147 us; the launch traced here: 146 us
  starting transfers between devices  92.3 us (63%)
  waiting for transfers between devices  36.6 us (25%)
  Pallas kernels  9.51 us (6%)
  other arithmetic  4.41 us (3%)
  local copies, waits for them, and re-layouts  3.05 us (2%)
    ppermute x6, starting transfers between devices, along_z(): return lax.ppermute(blocks, 'zl', [(i, i ^ step) for i in range(8)])  37 us
    ppermute x2, starting transfers between devices, summed(): got = lax.ppermute(theirs, 'zh', [(0, 1), (1, 0)])  25.5 us
    ppermute x6, waiting for transfers between devices, along_z(): return lax.ppermute(blocks, 'zl', [(i, i ^ step) for i in range(8)])  19.6 us
    all_to_all x2, waiting for transfers between devices, summed(): parts = lax.all_to_all(partial, ('x', 'y'), 0, 0)  12.4 us
    all_to_all x2, starting transfers between devices, summed(): parts = lax.all_to_all(partial, ('x', 'y'), 0, 0)  12.3 us
    ppermute x4, starting transfers between devices, other_core(): return lax.ppermute(blocks, 'core', [(0, 1), (1, 0)])  8.14 us
    pallas_call x2, Pallas kernels, product(): pl.pallas_call(functools.partial(product_kernel, row_count, count), grid=...  7.43 us
    all_to_all x1, starting transfers between devices, shards(): panel = lax.all_to_all(windows, 'y', 0, 0)  4.59 us
  transfers between devices with their start and end apart: 17, of which 8 were waited for; matrix products, arithmetic and copies ran while one was open for 5% of the time, Pallas kernels for 5%

profile of v2, /device:TPU:32, one launch (start us, length us, event | category | flops | bytes accessed | tf_op | source)
XLA Modules:
  0.0 146.2 jit_solution(5229171387163661318)
XLA Ops:
  0.0 2.1 %roll.1 = (bf16[1,2,32,1024]{3,2,1,0:T(8,128)(2,1)}, bf16[1,2,32,1024]{3,2,1,0:T(8,128)(2,1)}, bf16[96,512]{1,0:T(8,128)(2,1)}, bf16[96,512]{1,0:T(8,128)(2,1)}) custom-call(s32[32]{0:T(128)} %offsets_ref.5, bf16[3,32,1024]{2,1,0:T(8,128)(2,1)} %band_ref.1, bf16[32,1024]{1,0:T(8,128)(2,1)} %vec_ref.1, bf16[96,2048]{1,0:T(8,128)(2,1)} %fin_ref.1), custom_call_target="tpu_custom_call" | custom-call | tf_op jit(solution)/shard_map/roll/pallas_call | solution.py:80
  2.1 9.1 %collective-permute-start.2 = (bf16[1,2,32,1024]{3,2,1,0:T(8,128)(2,1)}, bf16[1,2,32,1024]{3,2,1,0:T(8,128)(2,1)S(1)}, u32[]{:S(2)}, u32[]{:S(2)}) collective-permute-start(bf16[1,2,32,1024]{3,2,1,0:T(8,128)(2,1)} %get-tuple-element.11), channel_id=1, source_target_pairs={{0,8},{2,10},{4,12},{6,14},{8,0},{10,2},{12,4},{14,6},{1,9},{3,11}... | collective-permute-start | bytes 393224 | tf_op jit(solution)/shard_map/ppermute | solution.py:89
  11.2 3.4 %collective-permute-start = (bf16[96,512]{1,0:T(8,128)(2,1)}, bf16[96,512]{1,0:T(8,128)(2,1)S(1)}, u32[]{:S(2)}, u32[]{:S(2)}) collective-permute-start(bf16[96,512]{1,0:T(8,128)(2,1)} %get-tuple-element.9), channel_id=1, source_target_pairs={{0,64},{64,128},{128,192},{192,256},{256,320},{320,384},{384,448},... | collective-permute-start | bytes 294920 | tf_op jit(solution)/shard_map/ppermute | solution.py:103
  14.6 1.3 collective-permute-start.1
  15.9 1.9 %collective-permute-start.8 = (bf16[1,2,32,1024]{3,2,1,0:T(8,128)(2,1)}, bf16[1,2,32,1024]{3,2,1,0:T(8,128)(2,1)S(1)}, u32[]{:S(2)}, u32[]{:S(2)}) collective-permute-start(bf16[1,2,32,1024]{3,2,1,0:T(8,128)(2,1)} %get-tuple-element.12), channel_id=1, source_target_pairs={{0,8},{2,10},{4,12},{6,14},{8,0},{10,2},{12,4},{14,6},{1,9},{3,11}... | collective-permute-start | bytes 393224 | tf_op jit(solution)/shard_map/ppermute | solution.py:89
  17.8 1.6 %constant_dynamic-update-slice_fusion.2 = (bf16[4,2,32,1024]{3,2,1,0:T(8,128)(2,1)S(1)}, bf16[4,2,32,1024]{3,2,1,0:T(8,128)(2,1)}) fusion(bf16[1,2,32,1024]{3,2,1,0:T(8,128)(2,1)} %get-tuple-element.11, bf16[1,2,32,1024]{3,2,1,0:T(8,128)(2,1)} %get-tuple-element.12), kind=kLoop, calls=%fused_computation.24 | loop fusion | bytes 524288
  19.4 1.1 collective-permute-done.2
  20.6 0.9 pad_maximum_fusion.3
  21.5 14.4 %collective-permute-start.3 = (bf16[2,2,32,1024]{3,2,1,0:T(8,128)(2,1)S(1)}, bf16[2,2,32,1024]{3,2,1,0:T(8,128)(2,1)S(1)}, u32[]{:S(2)}, u32[]{:S(2)}) collective-permute-start(bf16[2,2,32,1024]{3,2,1,0:T(8,128)(2,1)S(1)} %pad_maximum_fusion.3), channel_id=1, source_target_pairs={{0,4},{2,6},{4,0},{6,2},{8,12},{10,14},{12,8},{14,10},{1,5},{3,7},... | collective-permute-start | bytes 786440 | tf_op jit(solution)/shard_map/ppermute | solution.py:89
  36.1 11.9 %collective-permute-done.3 = bf16[2,2,32,1024]{3,2,1,0:T(8,128)(2,1)S(1)} collective-permute-done((bf16[2,2,32,1024]{3,2,1,0:T(8,128)(2,1)S(1)}, bf16[2,2,32,1024]{3,2,1,0:T(8,128)(2,1)S(1)}, u32[]{:S(2)}, u32[]{:S(2)}) %collective-permute-start.3) | collective-permute-done | bytes 262176 | tf_op jit(solution)/shard_map/ppermute | solution.py:89
  47.9 1.9 %collective-permute-start.5 = (bf16[4,2,32,1024]{3,2,1,0:T(8,128)(2,1)S(1)}, bf16[4,2,32,1024]{3,2,1,0:T(8,128)(2,1)S(1)}, u32[]{:S(2)}, u32[]{:S(2)}) collective-permute-start(bf16[4,2,32,1024]{3,2,1,0:T(8,128)(2,1)S(1)} %constant_dynamic-update-slice_fusion.refs_0_), channel_id=1, source_target_pairs={{0,2},{2,0},{4,6},{6,4},{8,10},{10,8},{12,14},{14,12},{1,3},{3,1},... | collective-permute-start | bytes 1572872 | tf_op jit(solution)/shard_map/ppermute | solution.py:89
  49.9 1.2 pad_maximum_fusion
  51.1 4.6 %all-to-all-start = ((bf16[4,96,1536]{2,1,0:T(8,128)(2,1)}), bf16[4,96,1536]{2,1,0:T(8,128)(2,1)S(1)}, u32[]{:S(2)}, u32[]{:S(2)}) async-start(bf16[4,96,1536]{2,1,0:T(8,128)(2,1)} %pad_maximum_fusion), calls=%async_computation | async-start | bytes 2359296 | tf_op jit(solution)/shard_map/all_to_all | solution.py:107
  55.7 5.3 %collective-permute-start.9 = (bf16[2,2,32,1024]{3,2,1,0:T(8,128)(2,1)S(1)}, bf16[2,2,32,1024]{3,2,1,0:T(8,128)(2,1)S(1)}, u32[]{:S(2)}, u32[]{:S(2)}) collective-permute-start(bf16[2,2,32,1024]{3,2,1,0:T(8,128)(2,1)S(1)} %pad_maximum_fusion.4), channel_id=1, source_target_pairs={{0,4},{2,6},{4,0},{6,2},{8,12},{10,14},{12,8},{14,10},{1,5},{3,7},... | collective-permute-start | bytes 786440 | tf_op jit(solution)/shard_map/ppermute | solution.py:89
  61.7 1.9 %collective-permute-start.4 = (bf16[4,2,32,1024]{3,2,1,0:T(8,128)(2,1)S(1)}, bf16[4,2,32,1024]{3,2,1,0:T(8,128)(2,1)S(1)}, u32[]{:S(2)}, u32[]{:S(2)}) collective-permute-start(bf16[4,2,32,1024]{3,2,1,0:T(8,128)(2,1)S(1)} %constant_dynamic-update-slice_fusion.refs_0_), channel_id=1, source_target_pairs={{0,1},{1,0},{2,3},{3,2},{4,5},{5,4},{6,7},{7,6},{8,9},{9,8},{10,11... | collective-permute-start | bytes 1572872 | tf_op jit(solution)/shard_map/ppermute | solution.py:92
  63.6 1.2 collective-permute-done.5.refs_2_
  64.8 1.9 %collective-permute-start.6 = (bf16[4,2,32,1024]{3,2,1,0:T(8,128)(2,1)S(1)}, bf16[4,2,32,1024]{3,2,1,0:T(8,128)(2,1)S(1)}, u32[]{:S(2)}, u32[]{:S(2)}) collective-permute-start(bf16[4,2,32,1024]{3,2,1,0:T(8,128)(2,1)S(1)} %collective-permute-done.5.refs_2_), channel_id=1, source_target_pairs={{0,1},{1,0},{2,3},{3,2},{4,5},{5,4},{6,7},{7,6},{8,9},{9,8},{10,11... | collective-permute-start | bytes 1572872 | tf_op jit(solution)/shard_map/ppermute | solution.py:92
  66.7 5.4 %collective-permute-done.9 = bf16[2,2,32,1024]{3,2,1,0:T(8,128)(2,1)S(1)} collective-permute-done((bf16[2,2,32,1024]{3,2,1,0:T(8,128)(2,1)S(1)}, bf16[2,2,32,1024]{3,2,1,0:T(8,128)(2,1)S(1)}, u32[]{:S(2)}, u32[]{:S(2)}) %collective-permute-start.9) | collective-permute-done | bytes 262176 | tf_op jit(solution)/shard_map/ppermute | solution.py:89
  72.8 4.4 %collective-permute-start.11 = (bf16[4,2,32,1024]{3,2,1,0:T(8,128)(2,1)}, bf16[4,2,32,1024]{3,2,1,0:T(8,128)(2,1)}, u32[]{:S(2)}, u32[]{:S(2)}) collective-permute-start(bf16[4,2,32,1024]{3,2,1,0:T(8,128)(2,1)} %constant_dynamic-update-slice_fusion.3.refs_4_), channel_id=1, source_target_pairs={{0,2},{2,0},{4,6},{6,4},{8,10},{10,8},{12,14},{14,12},{1,3},{3,1},... | collective-permute-start | bytes 1572872 | tf_op jit(solution)/shard_map/ppermute | solution.py:89
  77.3 2.7 %product_1.1 = bf16[16,1,2,96,128]{4,3,2,1,0:T(8,128)(2,1)} custom-call(s32[32]{0:T(128)S(1)} %copy-done, bf16[4,96,1536]{2,1,0:T(8,128)(2,1)S(1)} %all-to-all-done.panel_ref, bf16[4,2,32,1024]{3,2,1,0:T(8,128)(2,1)S(1)} %constant_dynamic-update-slice_fusion.refs_0_, bf16[4,2,32,1024]{3,2,1,0:T(8,128)(2,1)S(1)} %collective-permute-done.4.refs_1_, ...), custom_call_target="tpu_custom_call" | custom-call | flops 1006632960 | bytes 4000000 | tf_op jit(solution)/shard_map/product_1/pallas_call | solution.py:111
  80.0 6.8 %all-to-all-start.1 = ((bf16[16,1,2,96,128]{4,3,2,1,0:T(8,128)(2,1)}), bf16[16,1,2,96,128]{4,3,2,1,0:T(8,128)(2,1)}, u32[]{:S(2)}, u32[]{:S(2)}) async-start(bf16[16,1,2,96,128]{4,3,2,1,0:T(8,128)(2,1)} %product_1.1), calls=%async_computation.1 | async-start | bytes 1572864 | tf_op jit(solution)/shard_map/all_to_all | solution.py:128
  86.8 1.9 %collective-permute-start.10 = (bf16[4,2,32,1024]{3,2,1,0:T(8,128)(2,1)}, bf16[4,2,32,1024]{3,2,1,0:T(8,128)(2,1)S(1)}, u32[]{:S(2)}, u32[]{:S(2)}) collective-permute-start(bf16[4,2,32,1024]{3,2,1,0:T(8,128)(2,1)} %constant_dynamic-update-slice_fusion.3.refs_4_), channel_id=1, source_target_pairs={{0,1},{1,0},{2,3},{3,2},{4,5},{5,4},{6,7},{7,6},{8,9},{9,8},{10,11... | collective-permute-start | bytes 1572872 | tf_op jit(solution)/shard_map/ppermute | solution.py:92
  88.7 2.4 %collective-permute-start.12 = (bf16[4,2,32,1024]{3,2,1,0:T(8,128)(2,1)}, bf16[4,2,32,1024]{3,2,1,0:T(8,128)(2,1)S(1)}, u32[]{:S(2)}, u32[]{:S(2)}) collective-permute-start(bf16[4,2,32,1024]{3,2,1,0:T(8,128)(2,1)} %collective-permute-done.11.refs_6_), channel_id=1, source_target_pairs={{0,1},{1,0},{2,3},{3,2},{4,5},{5,4},{6,7},{7,6},{8,9},{9,8},{10,11... | collective-permute-start | bytes 1572872 | tf_op jit(solution)/shard_map/ppermute | solution.py:92
  91.2 1.7 %collective-permute-done.12.refs_7_ = bf16[4,2,32,1024]{3,2,1,0:T(8,128)(2,1)S(1)} collective-permute-done((bf16[4,2,32,1024]{3,2,1,0:T(8,128)(2,1)}, bf16[4,2,32,1024]{3,2,1,0:T(8,128)(2,1)S(1)}, u32[]{:S(2)}, u32[]{:S(2)}) %collective-permute-start.12) | collective-permute-done | bytes 524320 | tf_op jit(solution)/shard_map/ppermute | solution.py:92
  92.9 4.7 %product_2.1 = bf16[16,2,2,96,128]{4,3,2,1,0:T(8,128)(2,1)} custom-call(s32[32]{0:T(128)S(1)} %copy-done, bf16[4,96,1536]{2,1,0:T(8,128)(2,1)S(1)} %all-to-all-done.panel_ref, bf16[4,2,32,1024]{3,2,1,0:T(8,128)(2,1)S(1)} %constant_dynamic-update-slice_fusion.refs_0_, bf16[4,2,32,1024]{3,2,1,0:T(8,128)(2,1)S(1)} %collective-permute-done.4.refs_1_, ...), custom_call_target="tpu_custom_call" | custom-call | flops 2013265920 | bytes 8000000 | tf_op jit(solution)/shard_map/product_2/pallas_call | solution.py:111
  97.6 1.7 %all-to-all-done.1 = bf16[16,1,2,96,128]{4,3,2,1,0:T(8,128)(2,1)} async-done(((bf16[16,1,2,96,128]{4,3,2,1,0:T(8,128)(2,1)}), bf16[16,1,2,96,128]{4,3,2,1,0:T(8,128)(2,1)}, u32[]{:S(2)}, u32[]{:S(2)}) %all-to-all-start.1) | async-done | bytes 786464 | tf_op jit(solution)/shard_map/all_to_all | solution.py:128
  99.3 5.5 %all-to-all-start.2 = ((bf16[16,2,2,96,128]{4,3,2,1,0:T(8,128)(2,1)}), bf16[16,2,2,96,128]{4,3,2,1,0:T(8,128)(2,1)S(1)}, u32[]{:S(2)}, u32[]{:S(2)}) async-start(bf16[16,2,2,96,128]{4,3,2,1,0:T(8,128)(2,1)} %product_2.1), calls=%async_computation.2 | async-start | bytes 3145728 | tf_op jit(solution)/shard_map/all_to_all | solution.py:128
  104.8 1.3 convert_reduce_fusion.1
  106.1 12.8 %collective-permute-start.7 = (bf16[1,96,128]{2,1,0:T(8,128)(2,1)S(1)}, bf16[1,96,128]{2,1,0:T(8,128)(2,1)S(1)}, u32[]{:S(2)}, u32[]{:S(2)}) collective-permute-start(bf16[1,96,128]{2,1,0:T(8,128)(2,1)S(1)} %fusion.7), channel_id=1, source_target_pairs={{0,256},{256,0},{1,257},{257,1},{2,258},{258,2},{3,259},{259,3},{4... | collective-permute-start | bytes 73736 | tf_op jit(solution)/shard_map/ppermute | solution.py:132
  118.9 10.7 %all-to-all-done.2 = bf16[16,2,2,96,128]{4,3,2,1,0:T(8,128)(2,1)S(1)} async-done(((bf16[16,2,2,96,128]{4,3,2,1,0:T(8,128)(2,1)}), bf16[16,2,2,96,128]{4,3,2,1,0:T(8,128)(2,1)S(1)}, u32[]{:S(2)}, u32[]{:S(2)}) %all-to-all-start.2) | async-done | bytes 1572896 | tf_op jit(solution)/shard_map/all_to_all | solution.py:128
  129.8 12.8 %collective-permute-start.13 = (bf16[2,96,128]{2,1,0:T(8,128)(2,1)S(1)}, bf16[2,96,128]{2,1,0:T(8,128)(2,1)S(1)}, u32[]{:S(2)}, u32[]{:S(2)}) collective-permute-start(bf16[2,96,128]{2,1,0:T(8,128)(2,1)S(1)} %fusion.5), channel_id=1, source_target_pairs={{0,256},{256,0},{1,257},{257,1},{2,258},{258,2},{3,259},{259,3},{4... | collective-permute-start | bytes 147464 | tf_op jit(solution)/shard_map/ppermute | solution.py:132
  142.6 2.9 %collective-permute-done.13 = bf16[2,96,128]{2,1,0:T(8,128)(2,1)S(1)} collective-permute-done((bf16[2,96,128]{2,1,0:T(8,128)(2,1)S(1)}, bf16[2,96,128]{2,1,0:T(8,128)(2,1)S(1)}, u32[]{:S(2)}, u32[]{:S(2)}) %collective-permute-start.13) | collective-permute-done | bytes 49184 | tf_op jit(solution)/shard_map/ppermute | solution.py:132
  (27 shorter events, 2.5 us)
Async XLA Ops:
  0.0 35.9 %copy-start.1 = (bf16[96,2048]{1,0:T(8,128)(2,1)S(1)}, bf16[96,2048]{1,0:T(8,128)(2,1)}, u32[]{:S(2)}) copy-start(bf16[96,2048]{1,0:T(8,128)(2,1)} %fin_ref.1) | copy-start | bytes 1179652
  2.1 18.5 %collective-permute-start.2 = (bf16[1,2,32,1024]{3,2,1,0:T(8,128)(2,1)}, bf16[1,2,32,1024]{3,2,1,0:T(8,128)(2,1)S(1)}, u32[]{:S(2)}, u32[]{:S(2)}) collective-permute-start(bf16[1,2,32,1024]{3,2,1,0:T(8,128)(2,1)} %get-tuple-element.11), channel_id=1, source_target_pairs={{0,8},{2,10},{4,12},{6,14},{8,0},{10,2},{12,4},{14,6},{1,9},{3,11}... | collective-permute-start | bytes 393224 | tf_op jit(solution)/shard_map/ppermute | solution.py:89
  11.2 24.8 %collective-permute-start = (bf16[96,512]{1,0:T(8,128)(2,1)}, bf16[96,512]{1,0:T(8,128)(2,1)S(1)}, u32[]{:S(2)}, u32[]{:S(2)}) collective-permute-start(bf16[96,512]{1,0:T(8,128)(2,1)} %get-tuple-element.9), channel_id=1, source_target_pairs={{0,64},{64,128},{128,192},{192,256},{256,320},{320,384},{384,448},... | collective-permute-start | bytes 294920 | tf_op jit(solution)/shard_map/ppermute | solution.py:103
  14.6 21.4 %collective-permute-start.1 = (bf16[96,512]{1,0:T(8,128)(2,1)}, bf16[96,512]{1,0:T(8,128)(2,1)S(1)}, u32[]{:S(2)}, u32[]{:S(2)}) collective-permute-start(bf16[96,512]{1,0:T(8,128)(2,1)} %get-tuple-element.10), channel_id=1, source_target_pairs={{64,0},{128,64},{192,128},{256,192},{320,256},{384,320},{448,384},... | collective-permute-start | bytes 294920 | tf_op jit(solution)/shard_map/ppermute | solution.py:104
  15.9 39.8 %collective-permute-start.8 = (bf16[1,2,32,1024]{3,2,1,0:T(8,128)(2,1)}, bf16[1,2,32,1024]{3,2,1,0:T(8,128)(2,1)S(1)}, u32[]{:S(2)}, u32[]{:S(2)}) collective-permute-start(bf16[1,2,32,1024]{3,2,1,0:T(8,128)(2,1)} %get-tuple-element.12), channel_id=1, source_target_pairs={{0,8},{2,10},{4,12},{6,14},{8,0},{10,2},{12,4},{14,6},{1,9},{3,11}... | collective-permute-start | bytes 393224 | tf_op jit(solution)/shard_map/ppermute | solution.py:89
  21.5 26.4 %collective-permute-start.3 = (bf16[2,2,32,1024]{3,2,1,0:T(8,128)(2,1)S(1)}, bf16[2,2,32,1024]{3,2,1,0:T(8,128)(2,1)S(1)}, u32[]{:S(2)}, u32[]{:S(2)}) collective-permute-start(bf16[2,2,32,1024]{3,2,1,0:T(8,128)(2,1)S(1)} %pad_maximum_fusion.3), channel_id=1, source_target_pairs={{0,4},{2,6},{4,0},{6,2},{8,12},{10,14},{12,8},{14,10},{1,5},{3,7},... | collective-permute-start | bytes 786440 | tf_op jit(solution)/shard_map/ppermute | solution.py:89
  47.9 16.8 %collective-permute-start.5 = (bf16[4,2,32,1024]{3,2,1,0:T(8,128)(2,1)S(1)}, bf16[4,2,32,1024]{3,2,1,0:T(8,128)(2,1)S(1)}, u32[]{:S(2)}, u32[]{:S(2)}) collective-permute-start(bf16[4,2,32,1024]{3,2,1,0:T(8,128)(2,1)S(1)} %constant_dynamic-update-slice_fusion.refs_0_), channel_id=1, source_target_pairs={{0,2},{2,0},{4,6},{6,4},{8,10},{10,8},{12,14},{14,12},{1,3},{3,1},... | collective-permute-start | bytes 1572872 | tf_op jit(solution)/shard_map/ppermute | solution.py:89
  51.1 4.6 %copy-start.2 = (bf16[1,2,32,1024]{3,2,1,0:T(8,128)(2,1)S(1)}, bf16[1,2,32,1024]{3,2,1,0:T(8,128)(2,1)}, u32[]{:S(2)}) copy-start(bf16[1,2,32,1024]{3,2,1,0:T(8,128)(2,1)} %get-tuple-element.12) | copy-start | bytes 393220
  51.1 26.2 %all-to-all-start = ((bf16[4,96,1536]{2,1,0:T(8,128)(2,1)}), bf16[4,96,1536]{2,1,0:T(8,128)(2,1)S(1)}, u32[]{:S(2)}, u32[]{:S(2)}) async-start(bf16[4,96,1536]{2,1,0:T(8,128)(2,1)} %pad_maximum_fusion), calls=%async_computation | async-start | bytes 2359296 | tf_op jit(solution)/shard_map/all_to_all | solution.py:107
  55.7 21.6 %copy-start = (s32[32]{0:T(128)S(1)}, s32[32]{0:T(128)}, u32[]{:S(2)}) copy-start(s32[32]{0:T(128)} %offsets_ref.5) | copy-start | bytes 388
  55.7 16.4 %collective-permute-start.9 = (bf16[2,2,32,1024]{3,2,1,0:T(8,128)(2,1)S(1)}, bf16[2,2,32,1024]{3,2,1,0:T(8,128)(2,1)S(1)}, u32[]{:S(2)}, u32[]{:S(2)}) collective-permute-start(bf16[2,2,32,1024]{3,2,1,0:T(8,128)(2,1)S(1)} %pad_maximum_fusion.4), channel_id=1, source_target_pairs={{0,4},{2,6},{4,0},{6,2},{8,12},{10,14},{12,8},{14,10},{1,5},{3,7},... | collective-permute-start | bytes 786440 | tf_op jit(solution)/shard_map/ppermute | solution.py:89
  61.7 15.6 %collective-permute-start.4 = (bf16[4,2,32,1024]{3,2,1,0:T(8,128)(2,1)S(1)}, bf16[4,2,32,1024]{3,2,1,0:T(8,128)(2,1)S(1)}, u32[]{:S(2)}, u32[]{:S(2)}) collective-permute-start(bf16[4,2,32,1024]{3,2,1,0:T(8,128)(2,1)S(1)} %constant_dynamic-update-slice_fusion.refs_0_), channel_id=1, source_target_pairs={{0,1},{1,0},{2,3},{3,2},{4,5},{5,4},{6,7},{7,6},{8,9},{9,8},{10,11... | collective-permute-start | bytes 1572872 | tf_op jit(solution)/shard_map/ppermute | solution.py:92
  64.8 12.5 %collective-permute-start.6 = (bf16[4,2,32,1024]{3,2,1,0:T(8,128)(2,1)S(1)}, bf16[4,2,32,1024]{3,2,1,0:T(8,128)(2,1)S(1)}, u32[]{:S(2)}, u32[]{:S(2)}) collective-permute-start(bf16[4,2,32,1024]{3,2,1,0:T(8,128)(2,1)S(1)} %collective-permute-done.5.refs_2_), channel_id=1, source_target_pairs={{0,1},{1,0},{2,3},{3,2},{4,5},{5,4},{6,7},{7,6},{8,9},{9,8},{10,11... | collective-permute-start | bytes 1572872 | tf_op jit(solution)/shard_map/ppermute | solution.py:92
  72.8 15.9 %collective-permute-start.11 = (bf16[4,2,32,1024]{3,2,1,0:T(8,128)(2,1)}, bf16[4,2,32,1024]{3,2,1,0:T(8,128)(2,1)}, u32[]{:S(2)}, u32[]{:S(2)}) collective-permute-start(bf16[4,2,32,1024]{3,2,1,0:T(8,128)(2,1)} %constant_dynamic-update-slice_fusion.3.refs_4_), channel_id=1, source_target_pairs={{0,2},{2,0},{4,6},{6,4},{8,10},{10,8},{12,14},{14,12},{1,3},{3,1},... | collective-permute-start | bytes 1572872 | tf_op jit(solution)/shard_map/ppermute | solution.py:89
  80.0 19.3 %all-to-all-start.1 = ((bf16[16,1,2,96,128]{4,3,2,1,0:T(8,128)(2,1)}), bf16[16,1,2,96,128]{4,3,2,1,0:T(8,128)(2,1)}, u32[]{:S(2)}, u32[]{:S(2)}) async-start(bf16[16,1,2,96,128]{4,3,2,1,0:T(8,128)(2,1)} %product_1.1), calls=%async_computation.1 | async-start | bytes 1572864 | tf_op jit(solution)/shard_map/all_to_all | solution.py:128
  86.8 4.4 %collective-permute-start.10 = (bf16[4,2,32,1024]{3,2,1,0:T(8,128)(2,1)}, bf16[4,2,32,1024]{3,2,1,0:T(8,128)(2,1)S(1)}, u32[]{:S(2)}, u32[]{:S(2)}) collective-permute-start(bf16[4,2,32,1024]{3,2,1,0:T(8,128)(2,1)} %constant_dynamic-update-slice_fusion.3.refs_4_), channel_id=1, source_target_pairs={{0,1},{1,0},{2,3},{3,2},{4,5},{5,4},{6,7},{7,6},{8,9},{9,8},{10,11... | collective-permute-start | bytes 1572872 | tf_op jit(solution)/shard_map/ppermute | solution.py:92
  88.7 4.1 %collective-permute-start.12 = (bf16[4,2,32,1024]{3,2,1,0:T(8,128)(2,1)}, bf16[4,2,32,1024]{3,2,1,0:T(8,128)(2,1)S(1)}, u32[]{:S(2)}, u32[]{:S(2)}) collective-permute-start(bf16[4,2,32,1024]{3,2,1,0:T(8,128)(2,1)} %collective-permute-done.11.refs_6_), channel_id=1, source_target_pairs={{0,1},{1,0},{2,3},{3,2},{4,5},{5,4},{6,7},{7,6},{8,9},{9,8},{10,11... | collective-permute-start | bytes 1572872 | tf_op jit(solution)/shard_map/ppermute | solution.py:92
  99.3 30.3 %all-to-all-start.2 = ((bf16[16,2,2,96,128]{4,3,2,1,0:T(8,128)(2,1)}), bf16[16,2,2,96,128]{4,3,2,1,0:T(8,128)(2,1)S(1)}, u32[]{:S(2)}, u32[]{:S(2)}) async-start(bf16[16,2,2,96,128]{4,3,2,1,0:T(8,128)(2,1)} %product_2.1), calls=%async_computation.2 | async-start | bytes 3145728 | tf_op jit(solution)/shard_map/all_to_all | solution.py:128
  106.1 36.5 %collective-permute-start.7 = (bf16[1,96,128]{2,1,0:T(8,128)(2,1)S(1)}, bf16[1,96,128]{2,1,0:T(8,128)(2,1)S(1)}, u32[]{:S(2)}, u32[]{:S(2)}) collective-permute-start(bf16[1,96,128]{2,1,0:T(8,128)(2,1)S(1)} %fusion.7), channel_id=1, source_target_pairs={{0,256},{256,0},{1,257},{257,1},{2,258},{258,2},{3,259},{259,3},{4... | collective-permute-start | bytes 73736 | tf_op jit(solution)/shard_map/ppermute | solution.py:132
  129.8 15.7 %collective-permute-start.13 = (bf16[2,96,128]{2,1,0:T(8,128)(2,1)S(1)}, bf16[2,96,128]{2,1,0:T(8,128)(2,1)S(1)}, u32[]{:S(2)}, u32[]{:S(2)}) collective-permute-start(bf16[2,96,128]{2,1,0:T(8,128)(2,1)S(1)} %fusion.5), channel_id=1, source_target_pairs={{0,256},{256,0},{1,257},{257,1},{2,258},{258,2},{3,259},{259,3},{4... | collective-permute-start | bytes 147464 | tf_op jit(solution)/shard_map/ppermute | solution.py:132

commit v3 on v2

v3 whole, which is shorter than its diff:
```python
import functools

import jax
import jax.numpy as jnp
from jax import lax
from jax.experimental import pallas as pl
from jax.experimental.pallas import tpu as pltpu
from jax.sharding import Mesh
from jax.sharding import PartitionSpec as P

BLK = 64
HALF = 512
AXES = ("zh", "x", "y", "zl", "core")
ORDER = (0, 4, 2, 6, 1, 5, 3, 7)
VMEM = pl.BlockSpec(memory_space=pltpu.VMEM)
SMEM = pl.BlockSpec(memory_space=pltpu.SMEM)
SMALL = pltpu.CompilerParams(vmem_limit_bytes=4 * 1024 * 1024)


def panel_start(row_count):
    zh, x, y = (lax.axis_index(a) for a in AXES[:3])
    return (zh * 4 + x) * row_count + (y - 1) * HALF


def roll_kernel(offsets_ref, band_ref, vec_ref, fin_ref, own_ref, last_ref, first_ref):
    row_count = fin_ref.shape[1]
    start = offsets_ref[lax.axis_index("y") * 8 + lax.axis_index("zl")] - panel_start(row_count)

    def rolled(p):
        return pltpu.roll(band_ref[p].astype(jnp.float32), start, 1).astype(jnp.bfloat16)

    own_ref[0, 0] = vec_ref[...]
    for p in range(band_ref.shape[0]):
        own_ref[0, p + 1] = rolled(p)
    last_ref[...] = fin_ref[:, row_count - HALF :]
    first_ref[...] = fin_ref[:, :HALF]


def pair_kernel(own_ref, got_ref, before_ref, fin_ref, after_ref, two_ref, windows_ref):
    two_ref[:1] = own_ref[...]
    two_ref[1:] = got_ref[...]
    quarters = windows_ref.shape[0]
    for k in range(quarters):
        for c in range(3):
            source, at = fin_ref, k + c - 1
            if at < 0:
                source, at = before_ref, 0
            elif at == quarters:
                source, at = after_ref, 0
            windows_ref[k, :, c * HALF : (c + 1) * HALF] = source[:, at * HALF : (at + 1) * HALF]


def near_kernel(two_ref, more_ref, panel_ref, out_ref):
    out_ref[:2] = two_ref[...]
    out_ref[2:] = more_ref[...]


def product_kernel(row_count, first, offsets_ref, panel_ref, *refs):
    pieces, out_ref, band_s, vec_s = refs[:-3], refs[-3], refs[-2], refs[-1]
    p = pl.program_id(0) + first + 1
    blocks, _, rows, width = pieces[0].shape
    base, zl = lax.axis_index("y") * 8, lax.axis_index("zl")
    lane = lax.broadcasted_iota(jnp.int32, (rows, HALF), 1)
    for a in range(4):
        for n in range(blocks):
            at = pl.ds((a * blocks + n) * rows, rows)
            start = offsets_ref[base + (zl ^ ORDER[a // 2 * blocks + n])] - panel_start(row_count)
            low = pieces[a][n, p, :, :HALF]
            zero = jnp.zeros_like(low)
            band_s[at, :HALF] = jnp.where(lane >= start, low, zero)
            band_s[at, HALF:width] = pieces[a][n, p, :, HALF:]
            band_s[at, width:] = jnp.where(lane < start, low, zero)
            vec_s[at, :] = pieces[a][n, 0]
    quarters, lines = panel_ref.shape[:2]
    panel = panel_ref[...].reshape(quarters * lines, panel_ref.shape[2])
    applied = lax.dot_general(
        panel, band_s[...], (((1,), (1,)), ((), ())), preferred_element_type=jnp.float32
    ).astype(jnp.bfloat16)
    sums = jnp.dot(applied, vec_s[...], preferred_element_type=jnp.float32).astype(out_ref.dtype)
    lanes = out_ref.shape[-1]
    for dx in range(4):
        for dy in range(4):
            for dz in range(2):
                out_ref[dx * 4 + dy, 0, dz] = sums[
                    dy * lines : (dy + 1) * lines, (dz * 4 + dx) * lanes : (dz * 4 + dx + 1) * lanes
                ]


def shards(band_values, initial_vectors, final_vectors, band_offsets):
    comps, own_rows, width = band_values.shape
    lines, row_count = final_vectors.shape
    vectors = initial_vectors.shape[1]
    zh = lax.axis_index("zh")
    bf16 = jnp.bfloat16

    block = jax.ShapeDtypeStruct((1, comps + 1, own_rows, width), bf16)
    edge = jax.ShapeDtypeStruct((lines, HALF), bf16)
    own, last, first = pl.pallas_call(
        roll_kernel,
        out_shape=(block, edge, edge),
        in_specs=[SMEM, VMEM, VMEM, VMEM],
        out_specs=(VMEM, VMEM, VMEM),
        compiler_params=SMALL,
        name="roll",
    )(band_offsets, band_values, initial_vectors, final_vectors)

    def along_z(blocks, step):
        return lax.ppermute(blocks, "zl", [(i, i ^ step) for i in range(8)])

    def other_core(blocks):
        return lax.ppermute(blocks, "core", [(0, 1), (1, 0)])

    before = lax.ppermute(last, ("zh", "x"), [(i, i + 1) for i in range(7)])
    after = lax.ppermute(first, ("zh", "x"), [(i + 1, i) for i in range(7)])
    two, windows = pl.pallas_call(
        pair_kernel,
        out_shape=(
            jax.ShapeDtypeStruct((2, comps + 1, own_rows, width), bf16),
            jax.ShapeDtypeStruct((4, lines, 3 * HALF), bf16),
        ),
        in_specs=[VMEM] * 5,
        out_specs=(VMEM, VMEM),
        compiler_params=SMALL,
        name="pair",
    )(own, along_z(own, 4), before, final_vectors, after)
    panel = lax.all_to_all(windows, "y", 0, 0)

    near = pl.pallas_call(
        near_kernel,
        out_shape=jax.ShapeDtypeStruct((4, comps + 1, own_rows, width), bf16),
        in_specs=[VMEM, VMEM, VMEM],
        out_specs=VMEM,
        compiler_params=SMALL,
        name="near",
    )(two, along_z(two, 2), panel)
    far = along_z(near, 1)
    blocks = [near, other_core(near), far, other_core(far)]

    def product(first, count):
        depth = 16 * own_rows
        return pl.pallas_call(
            functools.partial(product_kernel, row_count, first),
            grid=(count,),
            out_shape=jax.ShapeDtypeStruct((16, count, 2, lines, vectors // 8), bf16),
            in_specs=[SMEM, VMEM] + [VMEM] * len(blocks),
            out_specs=pl.BlockSpec((16, 1, 2, lines, vectors // 8), lambda p: (0, p, 0, 0, 0)),
            scratch_shapes=[pltpu.VMEM((depth, 3 * HALF), bf16), pltpu.VMEM((depth, vectors), bf16)],
            compiler_params=pltpu.CompilerParams(vmem_limit_bytes=16 * 1024 * 1024),
            cost_estimate=pl.CostEstimate(
                flops=2 * count * 4 * lines * depth * (3 * HALF + vectors),
                bytes_accessed=4_000_000 * count,
                transcendentals=0,
            ),
            name=f"product_{count}",
        )(band_offsets, panel, *blocks)

    def summed(partial):
        parts = lax.all_to_all(partial, ("x", "y"), 0, 0)
        total = jnp.sum(parts.astype(jnp.float32), axis=0)
        mine = jnp.where(zh == 0, total[:, 0], total[:, 1])
        theirs = jnp.where(zh == 0, total[:, 1], total[:, 0]).astype(bf16)
        got = lax.ppermute(theirs, "zh", [(0, 1), (1, 0)])
        return (mine + got.astype(jnp.float32)).astype(bf16)

    first_sum = summed(product(0, 1))
    rest_sum = summed(product(1, 2))
    return jnp.concatenate([first_sum, rest_sum])


def solution(mesh):
    fine = Mesh(mesh.devices.reshape(2, 4, 4, 8, 2), AXES)
    cfg, col = AXES[:2], AXES[2:]
    placed = (P(None, AXES, None), P(AXES, None), P(col, cfg), P(cfg))
    return jax.shard_map(
        shards, mesh=fine, in_specs=placed, out_specs=P(None, col, cfg), check_vma=False
    )
```

time: 147 us -> 176 us (1.20)
  waiting for transfers between devices: 36.6 us -> 84.5 us
  starting transfers between devices: 92.3 us -> 70.8 us
  local copies, waits for them, and re-layouts: 3.05 us -> 9.98 us
  other arithmetic: 4.41 us -> 2.18 us
    ppermute x6 -> x3, waiting for transfers between devices: 19.6 us -> 50.3 us  [along_z(): return lax.ppermute(blocks, 'zl', [(i, i ^ step) for i in range(8)])]
    ppermute x6 -> x3, starting transfers between devices: 37 us -> 22.5 us  [along_z(): return lax.ppermute(blocks, 'zl', [(i, i ^ step) for i in range(8)])]
    all_to_all x2, waiting for transfers between devices: 12.4 us -> 20.2 us  [summed(): parts = lax.all_to_all(partial, ('x', 'y'), 0, 0)]
    unnamed x9 -> x22, local copies, waits for them, and re-layouts: 2.32 us -> 9.98 us
    ppermute x2, starting transfers between devices: 25.5 us -> 18 us  [summed(): got = lax.ppermute(theirs, 'zh', [(0, 1), (1, 0)])]
    all_to_all x2, starting transfers between devices: 12.3 us -> 17.3 us  [summed(): parts = lax.all_to_all(partial, ('x', 'y'), 0, 0)]
    ppermute x1, waiting for transfers between devices: 0.01 us -> 4.32 us  [shards(): after = lax.ppermute(first, ('zh', 'x'), [(i + 1, i) for i in range(7)])]
    ppermute x4 -> x2, starting transfers between devices: 8.14 us -> 3.83 us  [other_core(): return lax.ppermute(blocks, 'core', [(0, 1), (1, 0)])]
  transfers between devices with their start and end apart: 17 -> 12, of which waited for: 8 -> 9; matrix products, arithmetic and copies ran while one was open for 5% -> 1% of each run, Pallas kernels for 5% -> 2%
where the time goes in v3:
time: 176 us; the launch traced here: 175 us
  waiting for transfers between devices  84.5 us (48%)
  starting transfers between devices  70.8 us (40%)
  local copies, waits for them, and re-layouts  9.98 us (6%)
  Pallas kernels  7.86 us (4%)
  other arithmetic  2.18 us (1%)
    ppermute x3, waiting for transfers between devices, along_z(): return lax.ppermute(blocks, 'zl', [(i, i ^ step) for i in range(8)])  50.3 us
    ppermute x3, starting transfers between devices, along_z(): return lax.ppermute(blocks, 'zl', [(i, i ^ step) for i in range(8)])  22.5 us
    all_to_all x2, waiting for transfers between devices, summed(): parts = lax.all_to_all(partial, ('x', 'y'), 0, 0)  20.2 us
    ppermute x2, starting transfers between devices, summed(): got = lax.ppermute(theirs, 'zh', [(0, 1), (1, 0)])  18 us
    all_to_all x2, starting transfers between devices, summed(): parts = lax.all_to_all(partial, ('x', 'y'), 0, 0)  17.3 us
    unnamed x22, local copies, waits for them, and re-layouts  9.98 us
    ppermute x2, waiting for transfers between devices, summed(): got = lax.ppermute(theirs, 'zh', [(0, 1), (1, 0)])  6.17 us
    pallas_call x2, Pallas kernels, product(): pl.pallas_call(functools.partial(product_kernel, row_count, first), grid=...  5.94 us
  transfers between devices with their start and end apart: 12, of which 9 were waited for; matrix products, arithmetic and copies ran while one was open for 1% of the time, Pallas kernels for 2%

profile of v3, /device:TPU:32, one launch (start us, length us, event | category | flops | bytes accessed | tf_op | source)
XLA Modules:
  0.0 175.5 jit_solution(17521993903963734523)
XLA Ops:
  0.0 1.0 copy-done.1
  1.0 0.9 copy-done.7
  4.1 9.1 %collective-permute-start = (bf16[1,4,32,1024]{3,2,1,0:T(8,128)(2,1)S(1)}, bf16[1,4,32,1024]{3,2,1,0:T(8,128)(2,1)S(1)}, u32[]{:S(2)}, u32[]{:S(2)}) collective-permute-start(bf16[1,4,32,1024]{3,2,1,0:T(8,128)(2,1)S(1)} %get-tuple-element.10.own_ref), channel_id=1, source_target_pairs={{0,8},{2,10},{4,12},{6,14},{8,0},{10,2},{12,4},{14,6},{1,9},{3,11}... | collective-permute-start | bytes 786440 | tf_op jit(solution)/shard_map/ppermute | solution.py:108
  13.2 3.4 %collective-permute-start.1 = (bf16[96,512]{1,0:T(8,128)(2,1)S(1)}, bf16[96,512]{1,0:T(8,128)(2,1)S(1)}, u32[]{:S(2)}, u32[]{:S(2)}) collective-permute-start(bf16[96,512]{1,0:T(8,128)(2,1)S(1)} %get-tuple-element.11), channel_id=1, source_target_pairs={{0,64},{64,128},{128,192},{192,256},{256,320},{320,384},{384,448},... | collective-permute-start | bytes 294920 | tf_op jit(solution)/shard_map/ppermute | solution.py:113
  16.6 1.3 collective-permute-start.2
  18.8 4.3 %collective-permute-done.2.after_ref = bf16[96,512]{1,0:T(8,128)(2,1)S(1)} collective-permute-done((bf16[96,512]{1,0:T(8,128)(2,1)S(1)}, bf16[96,512]{1,0:T(8,128)(2,1)S(1)}, u32[]{:S(2)}, u32[]{:S(2)}) %collective-permute-start.2) | collective-permute-done | bytes 98336 | tf_op jit(solution)/shard_map/ppermute | solution.py:114
  23.2 7.7 %collective-permute-done.got_ref = bf16[1,4,32,1024]{3,2,1,0:T(8,128)(2,1)S(1)} collective-permute-done((bf16[1,4,32,1024]{3,2,1,0:T(8,128)(2,1)S(1)}, bf16[1,4,32,1024]{3,2,1,0:T(8,128)(2,1)S(1)}, u32[]{:S(2)}, u32[]{:S(2)}) %collective-permute-start) | collective-permute-done | bytes 262176 | tf_op jit(solution)/shard_map/ppermute | solution.py:108
  30.9 1.0 copy-done.2
  31.9 1.1 pair.1
  33.0 4.5 %all-to-all-start = ((bf16[4,96,1536]{2,1,0:T(8,128)(2,1)}), bf16[4,96,1536]{2,1,0:T(8,128)(2,1)S(1)}, u32[]{:S(2)}, u32[]{:S(2)}) async-start(bf16[4,96,1536]{2,1,0:T(8,128)(2,1)} %get-tuple-element.13), calls=%async_computation | async-start | bytes 2359296 | tf_op jit(solution)/shard_map/all_to_all | solution.py:126
  37.5 9.9 %collective-permute-start.3 = (bf16[2,4,32,1024]{3,2,1,0:T(8,128)(2,1)S(1)}, bf16[2,4,32,1024]{3,2,1,0:T(8,128)(2,1)S(1)}, u32[]{:S(2)}, u32[]{:S(2)}) collective-permute-start(bf16[2,4,32,1024]{3,2,1,0:T(8,128)(2,1)S(1)} %get-tuple-element.14.two_ref), channel_id=1, source_target_pairs={{0,4},{2,6},{4,0},{6,2},{8,12},{10,14},{12,8},{14,10},{1,5},{3,7},... | collective-permute-start | bytes 1572872 | tf_op jit(solution)/shard_map/ppermute | solution.py:108
  47.3 21.1 %collective-permute-done.3.more_ref = bf16[2,4,32,1024]{3,2,1,0:T(8,128)(2,1)S(1)} collective-permute-done((bf16[2,4,32,1024]{3,2,1,0:T(8,128)(2,1)S(1)}, bf16[2,4,32,1024]{3,2,1,0:T(8,128)(2,1)S(1)}, u32[]{:S(2)}, u32[]{:S(2)}) %collective-permute-start.3) | collective-permute-done | bytes 524320 | tf_op jit(solution)/shard_map/ppermute | solution.py:108
  68.5 3.5 %collective-permute-start.5 = (bf16[4,4,32,1024]{3,2,1,0:T(8,128)(2,1)S(1)}, bf16[4,4,32,1024]{3,2,1,0:T(8,128)(2,1)S(1)}, u32[]{:S(2)}, u32[]{:S(2)}) collective-permute-start(bf16[4,4,32,1024]{3,2,1,0:T(8,128)(2,1)S(1)} %near.1.refs_0_), channel_id=1, source_target_pairs={{0,2},{2,0},{4,6},{6,4},{8,10},{10,8},{12,14},{14,12},{1,3},{3,1},... | collective-permute-start | bytes 3145736 | tf_op jit(solution)/shard_map/ppermute | solution.py:108
  72.1 1.9 %collective-permute-start.4 = (bf16[4,4,32,1024]{3,2,1,0:T(8,128)(2,1)S(1)}, bf16[4,4,32,1024]{3,2,1,0:T(8,128)(2,1)S(1)}, u32[]{:S(2)}, u32[]{:S(2)}) collective-permute-start(bf16[4,4,32,1024]{3,2,1,0:T(8,128)(2,1)S(1)} %near.1.refs_0_), channel_id=1, source_target_pairs={{0,1},{1,0},{2,3},{3,2},{4,5},{5,4},{6,7},{7,6},{8,9},{9,8},{10,11... | collective-permute-start | bytes 3145736 | tf_op jit(solution)/shard_map/ppermute | solution.py:111
  74.0 21.5 %collective-permute-done.5.refs_2_ = bf16[4,4,32,1024]{3,2,1,0:T(8,128)(2,1)S(1)} collective-permute-done((bf16[4,4,32,1024]{3,2,1,0:T(8,128)(2,1)S(1)}, bf16[4,4,32,1024]{3,2,1,0:T(8,128)(2,1)S(1)}, u32[]{:S(2)}, u32[]{:S(2)}) %collective-permute-start.5) | collective-permute-done | bytes 1048608 | tf_op jit(solution)/shard_map/ppermute | solution.py:108
  95.5 1.9 %collective-permute-start.6 = (bf16[4,4,32,1024]{3,2,1,0:T(8,128)(2,1)S(1)}, bf16[4,4,32,1024]{3,2,1,0:T(8,128)(2,1)S(1)}, u32[]{:S(2)}, u32[]{:S(2)}) collective-permute-start(bf16[4,4,32,1024]{3,2,1,0:T(8,128)(2,1)S(1)} %collective-permute-done.5.refs_2_), channel_id=1, source_target_pairs={{0,1},{1,0},{2,3},{3,2},{4,5},{5,4},{6,7},{7,6},{8,9},{9,8},{10,11... | collective-permute-start | bytes 3145736 | tf_op jit(solution)/shard_map/ppermute | solution.py:111
  97.4 2.6 %collective-permute-done.6.refs_3_ = bf16[4,4,32,1024]{3,2,1,0:T(8,128)(2,1)S(1)} collective-permute-done((bf16[4,4,32,1024]{3,2,1,0:T(8,128)(2,1)S(1)}, bf16[4,4,32,1024]{3,2,1,0:T(8,128)(2,1)S(1)}, u32[]{:S(2)}, u32[]{:S(2)}) %collective-permute-start.6) | collective-permute-done | bytes 1048608 | tf_op jit(solution)/shard_map/ppermute | solution.py:111
  100.0 2.7 %product_1.1 = bf16[16,1,2,96,128]{4,3,2,1,0:T(8,128)(2,1)} custom-call(s32[32]{0:T(128)S(1)} %copy-done.10, bf16[4,96,1536]{2,1,0:T(8,128)(2,1)S(1)} %all-to-all-done.panel_ref, bf16[4,4,32,1024]{3,2,1,0:T(8,128)(2,1)S(1)} %near.1.refs_0_, bf16[4,4,32,1024]{3,2,1,0:T(8,128)(2,1)S(1)} %collective-permute-done.4.refs_1_, ...), custom_call_target="tpu_custom_call" | custom-call | flops 1006632960 | bytes 4000000 | tf_op jit(solution)/shard_map/product_1/pallas_call | solution.py:141
  102.8 1.0 copy-done.3
  103.8 1.0 copy-done.5
  104.7 13.6 %all-to-all-start.1 = ((bf16[16,1,2,96,128]{4,3,2,1,0:T(8,128)(2,1)}), bf16[16,1,2,96,128]{4,3,2,1,0:T(8,128)(2,1)}, u32[]{:S(2)}, u32[]{:S(2)}) async-start(bf16[16,1,2,96,128]{4,3,2,1,0:T(8,128)(2,1)} %product_1.1), calls=%async_computation.1 | async-start | bytes 1572864 | tf_op jit(solution)/shard_map/all_to_all | solution.py:158
  118.4 1.2 copy-done.4
  119.6 1.2 copy-done.6
  120.8 3.2 %product_2.1 = bf16[16,2,2,96,128]{4,3,2,1,0:T(8,128)(2,1)S(1)} custom-call(s32[32]{0:T(128)S(1)} %copy-done.10, bf16[4,96,1536]{2,1,0:T(8,128)(2,1)S(1)} %all-to-all-done.panel_ref, bf16[4,4,32,1024]{3,2,1,0:T(8,128)(2,1)S(1)} %near.1.refs_0_, bf16[4,4,32,1024]{3,2,1,0:T(8,128)(2,1)S(1)} %copy-done.4, ...), custom_call_target="tpu_custom_call" | custom-call | flops 2013265920 | bytes 8000000 | tf_op jit(solution)/shard_map/product_2/pallas_call | solution.py:141
  124.1 1.2 copy-done
  125.2 8.1 %all-to-all-done.1 = bf16[16,1,2,96,128]{4,3,2,1,0:T(8,128)(2,1)} async-done(((bf16[16,1,2,96,128]{4,3,2,1,0:T(8,128)(2,1)}), bf16[16,1,2,96,128]{4,3,2,1,0:T(8,128)(2,1)}, u32[]{:S(2)}, u32[]{:S(2)}) %all-to-all-start.1) | async-done | bytes 786464 | tf_op jit(solution)/shard_map/all_to_all | solution.py:158
  133.3 3.7 %all-to-all-start.2 = ((bf16[16,2,2,96,128]{4,3,2,1,0:T(8,128)(2,1)}), bf16[16,2,2,96,128]{4,3,2,1,0:T(8,128)(2,1)S(1)}, u32[]{:S(2)}, u32[]{:S(2)}) async-start(bf16[16,2,2,96,128]{4,3,2,1,0:T(8,128)(2,1)} %copy-done), calls=%async_computation.2 | async-start | bytes 3145728 | tf_op jit(solution)/shard_map/all_to_all | solution.py:158
  137.0 1.3 convert_reduce_fusion.1
  138.3 9.0 %collective-permute-start.7 = (bf16[1,96,128]{2,1,0:T(8,128)(2,1)S(1)}, bf16[1,96,128]{2,1,0:T(8,128)(2,1)S(1)}, u32[]{:S(2)}, u32[]{:S(2)}) collective-permute-start(bf16[1,96,128]{2,1,0:T(8,128)(2,1)S(1)} %fusion.5), channel_id=1, source_target_pairs={{0,256},{256,0},{1,257},{257,1},{2,258},{258,2},{3,259},{259,3},{4... | collective-permute-start | bytes 73736 | tf_op jit(solution)/shard_map/ppermute | solution.py:162
  147.3 12.1 %all-to-all-done.2 = bf16[16,2,2,96,128]{4,3,2,1,0:T(8,128)(2,1)S(1)} async-done(((bf16[16,2,2,96,128]{4,3,2,1,0:T(8,128)(2,1)}), bf16[16,2,2,96,128]{4,3,2,1,0:T(8,128)(2,1)S(1)}, u32[]{:S(2)}, u32[]{:S(2)}) %all-to-all-start.2) | async-done | bytes 1572896 | tf_op jit(solution)/shard_map/all_to_all | solution.py:158
  159.6 9.0 %collective-permute-start.8 = (bf16[2,96,128]{2,1,0:T(8,128)(2,1)S(1)}, bf16[2,96,128]{2,1,0:T(8,128)(2,1)S(1)}, u32[]{:S(2)}, u32[]{:S(2)}) collective-permute-start(bf16[2,96,128]{2,1,0:T(8,128)(2,1)S(1)} %fusion.3), channel_id=1, source_target_pairs={{0,256},{256,0},{1,257},{257,1},{2,258},{258,2},{3,259},{259,3},{4... | collective-permute-start | bytes 147464 | tf_op jit(solution)/shard_map/ppermute | solution.py:162
  168.6 6.2 %collective-permute-done.8 = bf16[2,96,128]{2,1,0:T(8,128)(2,1)S(1)} collective-permute-done((bf16[2,96,128]{2,1,0:T(8,128)(2,1)S(1)}, bf16[2,96,128]{2,1,0:T(8,128)(2,1)S(1)}, u32[]{:S(2)}, u32[]{:S(2)}) %collective-permute-start.8) | collective-permute-done | bytes 49184 | tf_op jit(solution)/shard_map/ppermute | solution.py:162
  (26 shorter events, 4.1 us)
Async XLA Ops:
  0.0 1.0 copy-start.1
  1.0 0.9 copy-start.7
  1.9 0.8 copy-start.8
  2.8 0.7 copy-start.9
  4.1 26.7 %collective-permute-start = (bf16[1,4,32,1024]{3,2,1,0:T(8,128)(2,1)S(1)}, bf16[1,4,32,1024]{3,2,1,0:T(8,128)(2,1)S(1)}, u32[]{:S(2)}, u32[]{:S(2)}) collective-permute-start(bf16[1,4,32,1024]{3,2,1,0:T(8,128)(2,1)S(1)} %get-tuple-element.10.own_ref), channel_id=1, source_target_pairs={{0,8},{2,10},{4,12},{6,14},{8,0},{10,2},{12,4},{14,6},{1,9},{3,11}... | collective-permute-start | bytes 786440 | tf_op jit(solution)/shard_map/ppermute | solution.py:108
  13.2 5.6 %collective-permute-start.1 = (bf16[96,512]{1,0:T(8,128)(2,1)S(1)}, bf16[96,512]{1,0:T(8,128)(2,1)S(1)}, u32[]{:S(2)}, u32[]{:S(2)}) collective-permute-start(bf16[96,512]{1,0:T(8,128)(2,1)S(1)} %get-tuple-element.11), channel_id=1, source_target_pairs={{0,64},{64,128},{128,192},{192,256},{256,320},{320,384},{384,448},... | collective-permute-start | bytes 294920 | tf_op jit(solution)/shard_map/ppermute | solution.py:113
  16.6 6.5 %collective-permute-start.2 = (bf16[96,512]{1,0:T(8,128)(2,1)S(1)}, bf16[96,512]{1,0:T(8,128)(2,1)S(1)}, u32[]{:S(2)}, u32[]{:S(2)}) collective-permute-start(bf16[96,512]{1,0:T(8,128)(2,1)S(1)} %get-tuple-element.12), channel_id=1, source_target_pairs={{64,0},{128,64},{192,128},{256,192},{320,256},{384,320},{448,384},... | collective-permute-start | bytes 294920 | tf_op jit(solution)/shard_map/ppermute | solution.py:114
  30.9 1.0 copy-start.2
  33.0 35.4 %all-to-all-start = ((bf16[4,96,1536]{2,1,0:T(8,128)(2,1)}), bf16[4,96,1536]{2,1,0:T(8,128)(2,1)S(1)}, u32[]{:S(2)}, u32[]{:S(2)}) async-start(bf16[4,96,1536]{2,1,0:T(8,128)(2,1)} %get-tuple-element.13), calls=%async_computation | async-start | bytes 2359296 | tf_op jit(solution)/shard_map/all_to_all | solution.py:126
  37.5 62.6 %copy-start.10 = (s32[32]{0:T(128)S(1)}, s32[32]{0:T(128)}, u32[]{:S(2)}) copy-start(s32[32]{0:T(128)} %offsets_ref.5) | copy-start | bytes 388
  37.5 31.0 %collective-permute-start.3 = (bf16[2,4,32,1024]{3,2,1,0:T(8,128)(2,1)S(1)}, bf16[2,4,32,1024]{3,2,1,0:T(8,128)(2,1)S(1)}, u32[]{:S(2)}, u32[]{:S(2)}) collective-permute-start(bf16[2,4,32,1024]{3,2,1,0:T(8,128)(2,1)S(1)} %get-tuple-element.14.two_ref), channel_id=1, source_target_pairs={{0,4},{2,6},{4,0},{6,2},{8,12},{10,14},{12,8},{14,10},{1,5},{3,7},... | collective-permute-start | bytes 1572872 | tf_op jit(solution)/shard_map/ppermute | solution.py:108
  68.5 27.0 %collective-permute-start.5 = (bf16[4,4,32,1024]{3,2,1,0:T(8,128)(2,1)S(1)}, bf16[4,4,32,1024]{3,2,1,0:T(8,128)(2,1)S(1)}, u32[]{:S(2)}, u32[]{:S(2)}) collective-permute-start(bf16[4,4,32,1024]{3,2,1,0:T(8,128)(2,1)S(1)} %near.1.refs_0_), channel_id=1, source_target_pairs={{0,2},{2,0},{4,6},{6,4},{8,10},{10,8},{12,14},{14,12},{1,3},{3,1},... | collective-permute-start | bytes 3145736 | tf_op jit(solution)/shard_map/ppermute | solution.py:108
  72.1 25.4 %collective-permute-start.4 = (bf16[4,4,32,1024]{3,2,1,0:T(8,128)(2,1)S(1)}, bf16[4,4,32,1024]{3,2,1,0:T(8,128)(2,1)S(1)}, u32[]{:S(2)}, u32[]{:S(2)}) collective-permute-start(bf16[4,4,32,1024]{3,2,1,0:T(8,128)(2,1)S(1)} %near.1.refs_0_), channel_id=1, source_target_pairs={{0,1},{1,0},{2,3},{3,2},{4,5},{5,4},{6,7},{7,6},{8,9},{9,8},{10,11... | collective-permute-start | bytes 3145736 | tf_op jit(solution)/shard_map/ppermute | solution.py:111
  95.5 4.5 %collective-permute-start.6 = (bf16[4,4,32,1024]{3,2,1,0:T(8,128)(2,1)S(1)}, bf16[4,4,32,1024]{3,2,1,0:T(8,128)(2,1)S(1)}, u32[]{:S(2)}, u32[]{:S(2)}) collective-permute-start(bf16[4,4,32,1024]{3,2,1,0:T(8,128)(2,1)S(1)} %collective-permute-done.5.refs_2_), channel_id=1, source_target_pairs={{0,1},{1,0},{2,3},{3,2},{4,5},{5,4},{6,7},{7,6},{8,9},{9,8},{10,11... | collective-permute-start | bytes 3145736 | tf_op jit(solution)/shard_map/ppermute | solution.py:111
  102.8 1.0 copy-start.3
  103.8 1.0 copy-start.5
  104.7 28.5 %all-to-all-start.1 = ((bf16[16,1,2,96,128]{4,3,2,1,0:T(8,128)(2,1)}), bf16[16,1,2,96,128]{4,3,2,1,0:T(8,128)(2,1)}, u32[]{:S(2)}, u32[]{:S(2)}) async-start(bf16[16,1,2,96,128]{4,3,2,1,0:T(8,128)(2,1)} %product_1.1), calls=%async_computation.1 | async-start | bytes 1572864 | tf_op jit(solution)/shard_map/all_to_all | solution.py:158
  118.3 1.2 copy-start.4
  119.6 1.2 copy-start.6
  124.0 1.2 copy-start
  133.3 26.1 %all-to-all-start.2 = ((bf16[16,2,2,96,128]{4,3,2,1,0:T(8,128)(2,1)}), bf16[16,2,2,96,128]{4,3,2,1,0:T(8,128)(2,1)S(1)}, u32[]{:S(2)}, u32[]{:S(2)}) async-start(bf16[16,2,2,96,128]{4,3,2,1,0:T(8,128)(2,1)} %copy-done), calls=%async_computation.2 | async-start | bytes 3145728 | tf_op jit(solution)/shard_map/all_to_all | solution.py:158
  138.3 30.4 %collective-permute-start.7 = (bf16[1,96,128]{2,1,0:T(8,128)(2,1)S(1)}, bf16[1,96,128]{2,1,0:T(8,128)(2,1)S(1)}, u32[]{:S(2)}, u32[]{:S(2)}) collective-permute-start(bf16[1,96,128]{2,1,0:T(8,128)(2,1)S(1)} %fusion.5), channel_id=1, source_target_pairs={{0,256},{256,0},{1,257},{257,1},{2,258},{258,2},{3,259},{259,3},{4... | collective-permute-start | bytes 73736 | tf_op jit(solution)/shard_map/ppermute | solution.py:162
  159.6 15.2 %collective-permute-start.8 = (bf16[2,96,128]{2,1,0:T(8,128)(2,1)S(1)}, bf16[2,96,128]{2,1,0:T(8,128)(2,1)S(1)}, u32[]{:S(2)}, u32[]{:S(2)}) collective-permute-start(bf16[2,96,128]{2,1,0:T(8,128)(2,1)S(1)} %fusion.3), channel_id=1, source_target_pairs={{0,256},{256,0},{1,257},{257,1},{2,258},{258,2},{3,259},{259,3},{4... | collective-permute-start | bytes 147464 | tf_op jit(solution)/shard_map/ppermute | solution.py:162

commit v4 on v2

--- a/solution.py
+++ b/solution.py
@@ -21,8 +21,7 @@
     return (zh * 4 + x) * row_count + (y - 1) * HALF
 
 
-def roll_kernel(offsets_ref, band_ref, vec_ref, fin_ref, head_ref, tail_ref, last_ref, first_ref):
-    row_count = fin_ref.shape[1]
+def roll_kernel(offsets_ref, band_ref, vec_ref, head_ref, tail_ref, *, row_count):
     start = offsets_ref[lax.axis_index("y") * 8 + lax.axis_index("zl")] - panel_start(row_count)
 
     def rolled(p):
@@ -32,8 +31,6 @@
     head_ref[0, 1] = rolled(0)
     tail_ref[0, 0] = rolled(1)
     tail_ref[0, 1] = rolled(2)
-    last_ref[...] = fin_ref[:, row_count - HALF :]
-    first_ref[...] = fin_ref[:, :HALF]
 
 
 def product_kernel(row_count, count, offsets_ref, panel_ref, *refs):
@@ -76,14 +73,13 @@
     bf16 = jnp.bfloat16
 
     half = jax.ShapeDtypeStruct((1, 2, own_rows, width), bf16)
-    edge = jax.ShapeDtypeStruct((lines, HALF), bf16)
-    head, tail, last, first = pl.pallas_call(
-        roll_kernel,
-        out_shape=(half, half, edge, edge),
-        in_specs=[SMEM, VMEM, VMEM, VMEM],
-        out_specs=(VMEM, VMEM, VMEM, VMEM),
+    head, tail = pl.pallas_call(
+        functools.partial(roll_kernel, row_count=row_count),
+        out_shape=(half, half),
+        in_specs=[SMEM, VMEM, VMEM],
+        out_specs=(VMEM, VMEM),
         name="roll",
-    )(band_offsets, band_values, initial_vectors, final_vectors)
+    )(band_offsets, band_values, initial_vectors)
 
     def along_z(blocks, step):
         return lax.ppermute(blocks, "zl", [(i, i ^ step) for i in range(8)])
@@ -100,6 +96,7 @@
     head_blocks = gathered(head)
     tail_blocks = gathered(tail)
 
+    last, first = final_vectors[:, row_count - HALF :], final_vectors[:, :HALF]
     before = lax.ppermute(last, ("zh", "x"), [(i, i + 1) for i in range(7)])
     after = lax.ppermute(first, ("zh", "x"), [(i + 1, i) for i in range(7)])
     wide = jnp.concatenate([before, final_vectors, after], axis=1)

time: 147 us -> 148 us (level)
  no operation moved by 1% of the time
where the time goes in v4:
time: 148 us; the launch traced here: 147 us
  starting transfers between devices  92.9 us (63%)
  waiting for transfers between devices  36 us (24%)
  Pallas kernels  9.21 us (6%)
  other arithmetic  4.4 us (3%)
  local copies, waits for them, and re-layouts  4.02 us (3%)
    ppermute x6, starting transfers between devices, along_z(): return lax.ppermute(blocks, 'zl', [(i, i ^ step) for i in range(8)])  37 us
    ppermute x2, starting transfers between devices, summed(): got = lax.ppermute(theirs, 'zh', [(0, 1), (1, 0)])  25.2 us
    ppermute x6, waiting for transfers between devices, along_z(): return lax.ppermute(blocks, 'zl', [(i, i ^ step) for i in range(8)])  18.6 us
    all_to_all x2, starting transfers between devices, summed(): parts = lax.all_to_all(partial, ('x', 'y'), 0, 0)  13.3 us
    all_to_all x2, waiting for transfers between devices, summed(): parts = lax.all_to_all(partial, ('x', 'y'), 0, 0)  12.6 us
    ppermute x4, starting transfers between devices, other_core(): return lax.ppermute(blocks, 'core', [(0, 1), (1, 0)])  8.14 us
    pallas_call x2, Pallas kernels, product(): pl.pallas_call(functools.partial(product_kernel, row_count, count), grid=...  7.41 us
    all_to_all x1, starting transfers between devices, shards(): panel = lax.all_to_all(windows, 'y', 0, 0)  4.59 us
  transfers between devices with their start and end apart: 17, of which 8 were waited for; matrix products, arithmetic and copies ran while one was open for 5% of the time, Pallas kernels for 5%

profile of v4, /device:TPU:32, one launch (start us, length us, event | category | flops | bytes accessed | tf_op | source)
XLA Modules:
  0.0 146.8 jit_solution(11461807378303647645)
XLA Ops:
  0.0 1.8 %roll.1 = (bf16[1,2,32,1024]{3,2,1,0:T(8,128)(2,1)}, bf16[1,2,32,1024]{3,2,1,0:T(8,128)(2,1)}) custom-call(s32[32]{0:T(128)} %offsets_ref.5, bf16[3,32,1024]{2,1,0:T(8,128)(2,1)} %band_ref.1, bf16[32,1024]{1,0:T(8,128)(2,1)} %vec_ref.1), custom_call_target="tpu_custom_call" | custom-call | tf_op jit(solution)/shard_map/roll/pallas_call | solution.py:76
  1.8 9.1 %collective-permute-start.2 = (bf16[1,2,32,1024]{3,2,1,0:T(8,128)(2,1)}, bf16[1,2,32,1024]{3,2,1,0:T(8,128)(2,1)S(1)}, u32[]{:S(2)}, u32[]{:S(2)}) collective-permute-start(bf16[1,2,32,1024]{3,2,1,0:T(8,128)(2,1)} %get-tuple-element.7), channel_id=1, source_target_pairs={{0,8},{2,10},{4,12},{6,14},{8,0},{10,2},{12,4},{14,6},{1,9},{3,11}... | collective-permute-start | bytes 393224 | tf_op jit(solution)/shard_map/ppermute | solution.py:85
  10.9 1.0 fusion.8
  11.9 3.4 %collective-permute-start = (bf16[96,512]{1,0:T(8,128)(2,1)S(1)}, bf16[96,512]{1,0:T(8,128)(2,1)S(1)}, u32[]{:S(2)}, u32[]{:S(2)}) collective-permute-start(bf16[96,512]{1,0:T(8,128)(2,1)S(1)} %get-tuple-element.13), channel_id=1, source_target_pairs={{0,64},{64,128},{128,192},{192,256},{256,320},{320,384},{384,448},... | collective-permute-start | bytes 294920 | tf_op jit(solution)/shard_map/ppermute | solution.py:100
  15.3 1.3 collective-permute-start.1
  16.6 1.9 %collective-permute-start.8 = (bf16[1,2,32,1024]{3,2,1,0:T(8,128)(2,1)}, bf16[1,2,32,1024]{3,2,1,0:T(8,128)(2,1)S(1)}, u32[]{:S(2)}, u32[]{:S(2)}) collective-permute-start(bf16[1,2,32,1024]{3,2,1,0:T(8,128)(2,1)} %get-tuple-element.8), channel_id=1, source_target_pairs={{0,8},{2,10},{4,12},{6,14},{8,0},{10,2},{12,4},{14,6},{1,9},{3,11}... | collective-permute-start | bytes 393224 | tf_op jit(solution)/shard_map/ppermute | solution.py:85
  18.5 1.6 %constant_dynamic-update-slice_fusion.2 = (bf16[4,2,32,1024]{3,2,1,0:T(8,128)(2,1)S(1)}, bf16[4,2,32,1024]{3,2,1,0:T(8,128)(2,1)}) fusion(bf16[1,2,32,1024]{3,2,1,0:T(8,128)(2,1)} %get-tuple-element.7, bf16[1,2,32,1024]{3,2,1,0:T(8,128)(2,1)} %get-tuple-element.8), kind=kLoop, calls=%fused_computation.24 | loop fusion | bytes 524288
  20.3 0.9 pad_maximum_fusion.3
  21.2 14.4 %collective-permute-start.3 = (bf16[2,2,32,1024]{3,2,1,0:T(8,128)(2,1)S(1)}, bf16[2,2,32,1024]{3,2,1,0:T(8,128)(2,1)S(1)}, u32[]{:S(2)}, u32[]{:S(2)}) collective-permute-start(bf16[2,2,32,1024]{3,2,1,0:T(8,128)(2,1)S(1)} %pad_maximum_fusion.3), channel_id=1, source_target_pairs={{0,4},{2,6},{4,0},{6,2},{8,12},{10,14},{12,8},{14,10},{1,5},{3,7},... | collective-permute-start | bytes 786440 | tf_op jit(solution)/shard_map/ppermute | solution.py:85
  35.8 11.9 %collective-permute-done.3 = bf16[2,2,32,1024]{3,2,1,0:T(8,128)(2,1)S(1)} collective-permute-done((bf16[2,2,32,1024]{3,2,1,0:T(8,128)(2,1)S(1)}, bf16[2,2,32,1024]{3,2,1,0:T(8,128)(2,1)S(1)}, u32[]{:S(2)}, u32[]{:S(2)}) %collective-permute-start.3) | collective-permute-done | bytes 262176 | tf_op jit(solution)/shard_map/ppermute | solution.py:85
  47.7 1.9 %collective-permute-start.5 = (bf16[4,2,32,1024]{3,2,1,0:T(8,128)(2,1)S(1)}, bf16[4,2,32,1024]{3,2,1,0:T(8,128)(2,1)S(1)}, u32[]{:S(2)}, u32[]{:S(2)}) collective-permute-start(bf16[4,2,32,1024]{3,2,1,0:T(8,128)(2,1)S(1)} %constant_dynamic-update-slice_fusion.refs_0_), channel_id=1, source_target_pairs={{0,2},{2,0},{4,6},{6,4},{8,10},{10,8},{12,14},{14,12},{1,3},{3,1},... | collective-permute-start | bytes 1572872 | tf_op jit(solution)/shard_map/ppermute | solution.py:85
  49.6 1.2 pad_maximum_fusion
  50.8 4.6 %all-to-all-start = ((bf16[4,96,1536]{2,1,0:T(8,128)(2,1)}), bf16[4,96,1536]{2,1,0:T(8,128)(2,1)S(1)}, u32[]{:S(2)}, u32[]{:S(2)}) async-start(bf16[4,96,1536]{2,1,0:T(8,128)(2,1)} %pad_maximum_fusion), calls=%async_computation | async-start | bytes 2359296 | tf_op jit(solution)/shard_map/all_to_all | solution.py:104
  55.4 5.3 %collective-permute-start.9 = (bf16[2,2,32,1024]{3,2,1,0:T(8,128)(2,1)S(1)}, bf16[2,2,32,1024]{3,2,1,0:T(8,128)(2,1)S(1)}, u32[]{:S(2)}, u32[]{:S(2)}) collective-permute-start(bf16[2,2,32,1024]{3,2,1,0:T(8,128)(2,1)S(1)} %pad_maximum_fusion.4), channel_id=1, source_target_pairs={{0,4},{2,6},{4,0},{6,2},{8,12},{10,14},{12,8},{14,10},{1,5},{3,7},... | collective-permute-start | bytes 786440 | tf_op jit(solution)/shard_map/ppermute | solution.py:85
  61.4 1.9 %collective-permute-start.4 = (bf16[4,2,32,1024]{3,2,1,0:T(8,128)(2,1)S(1)}, bf16[4,2,32,1024]{3,2,1,0:T(8,128)(2,1)S(1)}, u32[]{:S(2)}, u32[]{:S(2)}) collective-permute-start(bf16[4,2,32,1024]{3,2,1,0:T(8,128)(2,1)S(1)} %constant_dynamic-update-slice_fusion.refs_0_), channel_id=1, source_target_pairs={{0,1},{1,0},{2,3},{3,2},{4,5},{5,4},{6,7},{7,6},{8,9},{9,8},{10,11... | collective-permute-start | bytes 1572872 | tf_op jit(solution)/shard_map/ppermute | solution.py:88
  63.3 1.2 collective-permute-done.5.refs_2_
  64.5 1.9 %collective-permute-start.6 = (bf16[4,2,32,1024]{3,2,1,0:T(8,128)(2,1)S(1)}, bf16[4,2,32,1024]{3,2,1,0:T(8,128)(2,1)S(1)}, u32[]{:S(2)}, u32[]{:S(2)}) collective-permute-start(bf16[4,2,32,1024]{3,2,1,0:T(8,128)(2,1)S(1)} %collective-permute-done.5.refs_2_), channel_id=1, source_target_pairs={{0,1},{1,0},{2,3},{3,2},{4,5},{5,4},{6,7},{7,6},{8,9},{9,8},{10,11... | collective-permute-start | bytes 1572872 | tf_op jit(solution)/shard_map/ppermute | solution.py:88
  66.4 5.4 %collective-permute-done.9 = bf16[2,2,32,1024]{3,2,1,0:T(8,128)(2,1)S(1)} collective-permute-done((bf16[2,2,32,1024]{3,2,1,0:T(8,128)(2,1)S(1)}, bf16[2,2,32,1024]{3,2,1,0:T(8,128)(2,1)S(1)}, u32[]{:S(2)}, u32[]{:S(2)}) %collective-permute-start.9) | collective-permute-done | bytes 262176 | tf_op jit(solution)/shard_map/ppermute | solution.py:85
  72.5 4.4 %collective-permute-start.11 = (bf16[4,2,32,1024]{3,2,1,0:T(8,128)(2,1)}, bf16[4,2,32,1024]{3,2,1,0:T(8,128)(2,1)}, u32[]{:S(2)}, u32[]{:S(2)}) collective-permute-start(bf16[4,2,32,1024]{3,2,1,0:T(8,128)(2,1)} %constant_dynamic-update-slice_fusion.3.refs_4_), channel_id=1, source_target_pairs={{0,2},{2,0},{4,6},{6,4},{8,10},{10,8},{12,14},{14,12},{1,3},{3,1},... | collective-permute-start | bytes 1572872 | tf_op jit(solution)/shard_map/ppermute | solution.py:85
  77.0 2.7 %product_1.1 = bf16[16,1,2,96,128]{4,3,2,1,0:T(8,128)(2,1)} custom-call(s32[32]{0:T(128)S(1)} %copy-done, bf16[4,96,1536]{2,1,0:T(8,128)(2,1)S(1)} %all-to-all-done.panel_ref, bf16[4,2,32,1024]{3,2,1,0:T(8,128)(2,1)S(1)} %constant_dynamic-update-slice_fusion.refs_0_, bf16[4,2,32,1024]{3,2,1,0:T(8,128)(2,1)S(1)} %collective-permute-done.4.refs_1_, ...), custom_call_target="tpu_custom_call" | custom-call | flops 1006632960 | bytes 4000000 | tf_op jit(solution)/shard_map/product_1/pallas_call | solution.py:108
  79.7 7.8 %all-to-all-start.1 = ((bf16[16,1,2,96,128]{4,3,2,1,0:T(8,128)(2,1)}), bf16[16,1,2,96,128]{4,3,2,1,0:T(8,128)(2,1)}, u32[]{:S(2)}, u32[]{:S(2)}) async-start(bf16[16,1,2,96,128]{4,3,2,1,0:T(8,128)(2,1)} %product_1.1), calls=%async_computation.1 | async-start | bytes 1572864 | tf_op jit(solution)/shard_map/all_to_all | solution.py:125
  87.5 1.9 %collective-permute-start.10 = (bf16[4,2,32,1024]{3,2,1,0:T(8,128)(2,1)}, bf16[4,2,32,1024]{3,2,1,0:T(8,128)(2,1)S(1)}, u32[]{:S(2)}, u32[]{:S(2)}) collective-permute-start(bf16[4,2,32,1024]{3,2,1,0:T(8,128)(2,1)} %constant_dynamic-update-slice_fusion.3.refs_4_), channel_id=1, source_target_pairs={{0,1},{1,0},{2,3},{3,2},{4,5},{5,4},{6,7},{7,6},{8,9},{9,8},{10,11... | collective-permute-start | bytes 1572872 | tf_op jit(solution)/shard_map/ppermute | solution.py:88
  89.4 2.4 %collective-permute-start.12 = (bf16[4,2,32,1024]{3,2,1,0:T(8,128)(2,1)}, bf16[4,2,32,1024]{3,2,1,0:T(8,128)(2,1)S(1)}, u32[]{:S(2)}, u32[]{:S(2)}) collective-permute-start(bf16[4,2,32,1024]{3,2,1,0:T(8,128)(2,1)} %collective-permute-done.11.refs_6_), channel_id=1, source_target_pairs={{0,1},{1,0},{2,3},{3,2},{4,5},{5,4},{6,7},{7,6},{8,9},{9,8},{10,11... | collective-permute-start | bytes 1572872 | tf_op jit(solution)/shard_map/ppermute | solution.py:88
  91.9 1.7 %collective-permute-done.12.refs_7_ = bf16[4,2,32,1024]{3,2,1,0:T(8,128)(2,1)S(1)} collective-permute-done((bf16[4,2,32,1024]{3,2,1,0:T(8,128)(2,1)}, bf16[4,2,32,1024]{3,2,1,0:T(8,128)(2,1)S(1)}, u32[]{:S(2)}, u32[]{:S(2)}) %collective-permute-start.12) | collective-permute-done | bytes 524320 | tf_op jit(solution)/shard_map/ppermute | solution.py:88
  93.6 4.7 %product_2.1 = bf16[16,2,2,96,128]{4,3,2,1,0:T(8,128)(2,1)} custom-call(s32[32]{0:T(128)S(1)} %copy-done, bf16[4,96,1536]{2,1,0:T(8,128)(2,1)S(1)} %all-to-all-done.panel_ref, bf16[4,2,32,1024]{3,2,1,0:T(8,128)(2,1)S(1)} %constant_dynamic-update-slice_fusion.refs_0_, bf16[4,2,32,1024]{3,2,1,0:T(8,128)(2,1)S(1)} %collective-permute-done.4.refs_1_, ...), custom_call_target="tpu_custom_call" | custom-call | flops 2013265920 | bytes 8000000 | tf_op jit(solution)/shard_map/product_2/pallas_call | solution.py:108
  98.3 1.7 %all-to-all-done.1 = bf16[16,1,2,96,128]{4,3,2,1,0:T(8,128)(2,1)} async-done(((bf16[16,1,2,96,128]{4,3,2,1,0:T(8,128)(2,1)}), bf16[16,1,2,96,128]{4,3,2,1,0:T(8,128)(2,1)}, u32[]{:S(2)}, u32[]{:S(2)}) %all-to-all-start.1) | async-done | bytes 786464 | tf_op jit(solution)/shard_map/all_to_all | solution.py:125
  99.9 5.5 %all-to-all-start.2 = ((bf16[16,2,2,96,128]{4,3,2,1,0:T(8,128)(2,1)}), bf16[16,2,2,96,128]{4,3,2,1,0:T(8,128)(2,1)S(1)}, u32[]{:S(2)}, u32[]{:S(2)}) async-start(bf16[16,2,2,96,128]{4,3,2,1,0:T(8,128)(2,1)} %product_2.1), calls=%async_computation.2 | async-start | bytes 3145728 | tf_op jit(solution)/shard_map/all_to_all | solution.py:125
  105.5 1.3 convert_reduce_fusion.1
  106.7 12.6 %collective-permute-start.7 = (bf16[1,96,128]{2,1,0:T(8,128)(2,1)S(1)}, bf16[1,96,128]{2,1,0:T(8,128)(2,1)S(1)}, u32[]{:S(2)}, u32[]{:S(2)}) collective-permute-start(bf16[1,96,128]{2,1,0:T(8,128)(2,1)S(1)} %fusion.7), channel_id=1, source_target_pairs={{0,256},{256,0},{1,257},{257,1},{2,258},{258,2},{3,259},{259,3},{4... | collective-permute-start | bytes 73736 | tf_op jit(solution)/shard_map/ppermute | solution.py:129
  119.3 10.9 %all-to-all-done.2 = bf16[16,2,2,96,128]{4,3,2,1,0:T(8,128)(2,1)S(1)} async-done(((bf16[16,2,2,96,128]{4,3,2,1,0:T(8,128)(2,1)}), bf16[16,2,2,96,128]{4,3,2,1,0:T(8,128)(2,1)S(1)}, u32[]{:S(2)}, u32[]{:S(2)}) %all-to-all-start.2) | async-done | bytes 1572896 | tf_op jit(solution)/shard_map/all_to_all | solution.py:125
  130.5 12.6 %collective-permute-start.13 = (bf16[2,96,128]{2,1,0:T(8,128)(2,1)S(1)}, bf16[2,96,128]{2,1,0:T(8,128)(2,1)S(1)}, u32[]{:S(2)}, u32[]{:S(2)}) collective-permute-start(bf16[2,96,128]{2,1,0:T(8,128)(2,1)S(1)} %fusion.5), channel_id=1, source_target_pairs={{0,256},{256,0},{1,257},{257,1},{2,258},{258,2},{3,259},{259,3},{4... | collective-permute-start | bytes 147464 | tf_op jit(solution)/shard_map/ppermute | solution.py:129
  143.1 3.1 %collective-permute-done.13 = bf16[2,96,128]{2,1,0:T(8,128)(2,1)S(1)} collective-permute-done((bf16[2,96,128]{2,1,0:T(8,128)(2,1)S(1)}, bf16[2,96,128]{2,1,0:T(8,128)(2,1)S(1)}, u32[]{:S(2)}, u32[]{:S(2)}) %collective-permute-start.13) | collective-permute-done | bytes 49184 | tf_op jit(solution)/shard_map/ppermute | solution.py:129
  (28 shorter events, 2.6 us)
Async XLA Ops:
  0.0 35.7 %copy-start.1 = (bf16[96,2048]{1,0:T(8,128)(2,1)S(1)}, bf16[96,2048]{1,0:T(8,128)(2,1)}, u32[]{:S(2)}) copy-start(bf16[96,2048]{1,0:T(8,128)(2,1)} %param.6) | copy-start | bytes 1179652
  1.8 18.5 %collective-permute-start.2 = (bf16[1,2,32,1024]{3,2,1,0:T(8,128)(2,1)}, bf16[1,2,32,1024]{3,2,1,0:T(8,128)(2,1)S(1)}, u32[]{:S(2)}, u32[]{:S(2)}) collective-permute-start(bf16[1,2,32,1024]{3,2,1,0:T(8,128)(2,1)} %get-tuple-element.7), channel_id=1, source_target_pairs={{0,8},{2,10},{4,12},{6,14},{8,0},{10,2},{12,4},{14,6},{1,9},{3,11}... | collective-permute-start | bytes 393224 | tf_op jit(solution)/shard_map/ppermute | solution.py:85
  11.9 23.8 %collective-permute-start = (bf16[96,512]{1,0:T(8,128)(2,1)S(1)}, bf16[96,512]{1,0:T(8,128)(2,1)S(1)}, u32[]{:S(2)}, u32[]{:S(2)}) collective-permute-start(bf16[96,512]{1,0:T(8,128)(2,1)S(1)} %get-tuple-element.13), channel_id=1, source_target_pairs={{0,64},{64,128},{128,192},{192,256},{256,320},{320,384},{384,448},... | collective-permute-start | bytes 294920 | tf_op jit(solution)/shard_map/ppermute | solution.py:100
  15.3 20.4 %collective-permute-start.1 = (bf16[96,512]{1,0:T(8,128)(2,1)S(1)}, bf16[96,512]{1,0:T(8,128)(2,1)S(1)}, u32[]{:S(2)}, u32[]{:S(2)}) collective-permute-start(bf16[96,512]{1,0:T(8,128)(2,1)S(1)} %get-tuple-element.14), channel_id=1, source_target_pairs={{64,0},{128,64},{192,128},{256,192},{320,256},{384,320},{448,384},... | collective-permute-start | bytes 294920 | tf_op jit(solution)/shard_map/ppermute | solution.py:101
  16.6 38.8 %collective-permute-start.8 = (bf16[1,2,32,1024]{3,2,1,0:T(8,128)(2,1)}, bf16[1,2,32,1024]{3,2,1,0:T(8,128)(2,1)S(1)}, u32[]{:S(2)}, u32[]{:S(2)}) collective-permute-start(bf16[1,2,32,1024]{3,2,1,0:T(8,128)(2,1)} %get-tuple-element.8), channel_id=1, source_target_pairs={{0,8},{2,10},{4,12},{6,14},{8,0},{10,2},{12,4},{14,6},{1,9},{3,11}... | collective-permute-start | bytes 393224 | tf_op jit(solution)/shard_map/ppermute | solution.py:85
  21.2 26.4 %collective-permute-start.3 = (bf16[2,2,32,1024]{3,2,1,0:T(8,128)(2,1)S(1)}, bf16[2,2,32,1024]{3,2,1,0:T(8,128)(2,1)S(1)}, u32[]{:S(2)}, u32[]{:S(2)}) collective-permute-start(bf16[2,2,32,1024]{3,2,1,0:T(8,128)(2,1)S(1)} %pad_maximum_fusion.3), channel_id=1, source_target_pairs={{0,4},{2,6},{4,0},{6,2},{8,12},{10,14},{12,8},{14,10},{1,5},{3,7},... | collective-permute-start | bytes 786440 | tf_op jit(solution)/shard_map/ppermute | solution.py:85
  47.7 16.8 %collective-permute-start.5 = (bf16[4,2,32,1024]{3,2,1,0:T(8,128)(2,1)S(1)}, bf16[4,2,32,1024]{3,2,1,0:T(8,128)(2,1)S(1)}, u32[]{:S(2)}, u32[]{:S(2)}) collective-permute-start(bf16[4,2,32,1024]{3,2,1,0:T(8,128)(2,1)S(1)} %constant_dynamic-update-slice_fusion.refs_0_), channel_id=1, source_target_pairs={{0,2},{2,0},{4,6},{6,4},{8,10},{10,8},{12,14},{14,12},{1,3},{3,1},... | collective-permute-start | bytes 1572872 | tf_op jit(solution)/shard_map/ppermute | solution.py:85
  50.8 4.6 %copy-start.2 = (bf16[1,2,32,1024]{3,2,1,0:T(8,128)(2,1)S(1)}, bf16[1,2,32,1024]{3,2,1,0:T(8,128)(2,1)}, u32[]{:S(2)}) copy-start(bf16[1,2,32,1024]{3,2,1,0:T(8,128)(2,1)} %get-tuple-element.8) | copy-start | bytes 393220
  50.8 26.2 %all-to-all-start = ((bf16[4,96,1536]{2,1,0:T(8,128)(2,1)}), bf16[4,96,1536]{2,1,0:T(8,128)(2,1)S(1)}, u32[]{:S(2)}, u32[]{:S(2)}) async-start(bf16[4,96,1536]{2,1,0:T(8,128)(2,1)} %pad_maximum_fusion), calls=%async_computation | async-start | bytes 2359296 | tf_op jit(solution)/shard_map/all_to_all | solution.py:104
  55.4 21.6 %copy-start = (s32[32]{0:T(128)S(1)}, s32[32]{0:T(128)}, u32[]{:S(2)}) copy-start(s32[32]{0:T(128)} %offsets_ref.5) | copy-start | bytes 388
  55.4 16.4 %collective-permute-start.9 = (bf16[2,2,32,1024]{3,2,1,0:T(8,128)(2,1)S(1)}, bf16[2,2,32,1024]{3,2,1,0:T(8,128)(2,1)S(1)}, u32[]{:S(2)}, u32[]{:S(2)}) collective-permute-start(bf16[2,2,32,1024]{3,2,1,0:T(8,128)(2,1)S(1)} %pad_maximum_fusion.4), channel_id=1, source_target_pairs={{0,4},{2,6},{4,0},{6,2},{8,12},{10,14},{12,8},{14,10},{1,5},{3,7},... | collective-permute-start | bytes 786440 | tf_op jit(solution)/shard_map/ppermute | solution.py:85
  61.4 15.5 %collective-permute-start.4 = (bf16[4,2,32,1024]{3,2,1,0:T(8,128)(2,1)S(1)}, bf16[4,2,32,1024]{3,2,1,0:T(8,128)(2,1)S(1)}, u32[]{:S(2)}, u32[]{:S(2)}) collective-permute-start(bf16[4,2,32,1024]{3,2,1,0:T(8,128)(2,1)S(1)} %constant_dynamic-update-slice_fusion.refs_0_), channel_id=1, source_target_pairs={{0,1},{1,0},{2,3},{3,2},{4,5},{5,4},{6,7},{7,6},{8,9},{9,8},{10,11... | collective-permute-start | bytes 1572872 | tf_op jit(solution)/shard_map/ppermute | solution.py:88
  64.5 12.5 %collective-permute-start.6 = (bf16[4,2,32,1024]{3,2,1,0:T(8,128)(2,1)S(1)}, bf16[4,2,32,1024]{3,2,1,0:T(8,128)(2,1)S(1)}, u32[]{:S(2)}, u32[]{:S(2)}) collective-permute-start(bf16[4,2,32,1024]{3,2,1,0:T(8,128)(2,1)S(1)} %collective-permute-done.5.refs_2_), channel_id=1, source_target_pairs={{0,1},{1,0},{2,3},{3,2},{4,5},{5,4},{6,7},{7,6},{8,9},{9,8},{10,11... | collective-permute-start | bytes 1572872 | tf_op jit(solution)/shard_map/ppermute | solution.py:88
  72.5 16.9 %collective-permute-start.11 = (bf16[4,2,32,1024]{3,2,1,0:T(8,128)(2,1)}, bf16[4,2,32,1024]{3,2,1,0:T(8,128)(2,1)}, u32[]{:S(2)}, u32[]{:S(2)}) collective-permute-start(bf16[4,2,32,1024]{3,2,1,0:T(8,128)(2,1)} %constant_dynamic-update-slice_fusion.3.refs_4_), channel_id=1, source_target_pairs={{0,2},{2,0},{4,6},{6,4},{8,10},{10,8},{12,14},{14,12},{1,3},{3,1},... | collective-permute-start | bytes 1572872 | tf_op jit(solution)/shard_map/ppermute | solution.py:85
  79.7 20.3 %all-to-all-start.1 = ((bf16[16,1,2,96,128]{4,3,2,1,0:T(8,128)(2,1)}), bf16[16,1,2,96,128]{4,3,2,1,0:T(8,128)(2,1)}, u32[]{:S(2)}, u32[]{:S(2)}) async-start(bf16[16,1,2,96,128]{4,3,2,1,0:T(8,128)(2,1)} %product_1.1), calls=%async_computation.1 | async-start | bytes 1572864 | tf_op jit(solution)/shard_map/all_to_all | solution.py:125
  87.5 4.4 %collective-permute-start.10 = (bf16[4,2,32,1024]{3,2,1,0:T(8,128)(2,1)}, bf16[4,2,32,1024]{3,2,1,0:T(8,128)(2,1)S(1)}, u32[]{:S(2)}, u32[]{:S(2)}) collective-permute-start(bf16[4,2,32,1024]{3,2,1,0:T(8,128)(2,1)} %constant_dynamic-update-slice_fusion.3.refs_4_), channel_id=1, source_target_pairs={{0,1},{1,0},{2,3},{3,2},{4,5},{5,4},{6,7},{7,6},{8,9},{9,8},{10,11... | collective-permute-start | bytes 1572872 | tf_op jit(solution)/shard_map/ppermute | solution.py:88
  89.4 4.1 %collective-permute-start.12 = (bf16[4,2,32,1024]{3,2,1,0:T(8,128)(2,1)}, bf16[4,2,32,1024]{3,2,1,0:T(8,128)(2,1)S(1)}, u32[]{:S(2)}, u32[]{:S(2)}) collective-permute-start(bf16[4,2,32,1024]{3,2,1,0:T(8,128)(2,1)} %collective-permute-done.11.refs_6_), channel_id=1, source_target_pairs={{0,1},{1,0},{2,3},{3,2},{4,5},{5,4},{6,7},{7,6},{8,9},{9,8},{10,11... | collective-permute-start | bytes 1572872 | tf_op jit(solution)/shard_map/ppermute | solution.py:88
  99.9 30.3 %all-to-all-start.2 = ((bf16[16,2,2,96,128]{4,3,2,1,0:T(8,128)(2,1)}), bf16[16,2,2,96,128]{4,3,2,1,0:T(8,128)(2,1)S(1)}, u32[]{:S(2)}, u32[]{:S(2)}) async-start(bf16[16,2,2,96,128]{4,3,2,1,0:T(8,128)(2,1)} %product_2.1), calls=%async_computation.2 | async-start | bytes 3145728 | tf_op jit(solution)/shard_map/all_to_all | solution.py:125
  106.7 36.3 %collective-permute-start.7 = (bf16[1,96,128]{2,1,0:T(8,128)(2,1)S(1)}, bf16[1,96,128]{2,1,0:T(8,128)(2,1)S(1)}, u32[]{:S(2)}, u32[]{:S(2)}) collective-permute-start(bf16[1,96,128]{2,1,0:T(8,128)(2,1)S(1)} %fusion.7), channel_id=1, source_target_pairs={{0,256},{256,0},{1,257},{257,1},{2,258},{258,2},{3,259},{259,3},{4... | collective-permute-start | bytes 73736 | tf_op jit(solution)/shard_map/ppermute | solution.py:129
  130.5 15.7 %collective-permute-start.13 = (bf16[2,96,128]{2,1,0:T(8,128)(2,1)S(1)}, bf16[2,96,128]{2,1,0:T(8,128)(2,1)S(1)}, u32[]{:S(2)}, u32[]{:S(2)}) collective-permute-start(bf16[2,96,128]{2,1,0:T(8,128)(2,1)S(1)} %fusion.5), channel_id=1, source_target_pairs={{0,256},{256,0},{1,257},{257,1},{2,258},{258,2},{3,259},{259,3},{4... | collective-permute-start | bytes 147464 | tf_op jit(solution)/shard_map/ppermute | solution.py:129
